TPU v7x, 32 devices: a whole 2x2x4 slice. The times are simulated.
32 devices in a mesh: ctx: 8 (over y, x, core), head: 4 (over z).
Axes of the slice: x: 2, y: 2, z: 4, core: 2. Of those that a mesh axis runs over, the one named last changes fastest.
Arguments:
- queries: bfloat16 [2048, 4096], P('ctx', 'head'), may hold values from -100 to 100
- keys: bfloat16 [16384, 4096], P('ctx', 'head'), may hold values from -4 to 4
- values: bfloat16 [16384, 4096], P('ctx', 'head'), may hold values from -6 to 6
- lengths: int32 [64], P('ctx'), may hold values from 1 to 256, as said below
- out_weight: bfloat16 [4096, 4096], P('head'), may hold values from -0.09375 to 0.09375
Outputs:
- layer_out: float32 [2048, 4096], P('ctx', 'head')
Inputs may be any that keep to these rules, and one draw needn't show every extreme that they name: `lengths`: each passage has at least one valid token; some passage is full and some has exactly one.
All inputs are finite; a program needn't handle non-finite values.
Results may differ from a plain program's by a relative error of at most 0.005.
Values may be sent and summed in bfloat16 or wider, within the bound.
No kernel may reach another device: no remote copies, remote signals or barrier semaphores. Data moves between devices by JAX's collectives and lax.ppermute only.
A program may use at most 192 MiB of HBM per device.

v0:
```python
import math

import jax
import jax.numpy as jnp
from jax import lax
from jax.sharding import PartitionSpec as P

HD = 128
SPAN = 256


def on_device(queries, keys, values, lengths, out_weight):
    whole = lax.all_gather(queries, "ctx", axis=0, tiled=True)
    row_count = whole.shape[0]
    local_ctx = keys.shape[0]
    heads_here = keys.shape[1] // HD
    positions = jnp.arange(local_ctx, dtype=jnp.int32)
    limits = jnp.repeat(lengths, SPAN, total_repeat_length=local_ctx)
    mask_bias = jnp.where(positions % SPAN < limits, 0.0, -1e30).astype(jnp.float32)
    score_scale = 1.0 / math.sqrt(HD)
    key_heads = keys.reshape(local_ctx, heads_here, HD)
    value_heads = values.reshape(local_ctx, heads_here, HD)
    row_block = min(512, row_count)
    row_steps = row_count // row_block
    query_blocks = whole.reshape(row_steps, row_block, heads_here, HD)
    sources = lax.axis_size("ctx")
    own_rows = row_count // sources

    def scores_of(query_rows):
        scores = jnp.einsum(
            "ihd,jhd->hij", query_rows, key_heads, preferred_element_type=jnp.float32
        )
        return scores * score_scale + mask_bias[None, None, :]

    def weigh(scores, shift):
        raised = jnp.exp(scores - shift[:, :, None])
        totals = jnp.sum(raised, axis=2)
        weighted = jnp.einsum(
            "hij,jhd->ihd",
            raised.astype(jnp.bfloat16),
            value_heads,
            preferred_element_type=jnp.float32,
        )
        return (weighted.reshape(row_block, heads_here * HD), totals.T)

    def partial_block(query_rows):
        scores = scores_of(query_rows)
        row_max = jnp.max(scores, axis=2)
        weighted, totals = weigh(scores, row_max)
        return (weighted, row_max.T, totals)

    weighted, maxima, totals = lax.map(partial_block, query_blocks)
    weighted = weighted.reshape(row_count, heads_here * HD)
    maxima = maxima.reshape(row_count, heads_here)
    totals = totals.reshape(row_count, heads_here)
    weighted, maxima, totals = (
        lax.all_to_all(weighted, "ctx", split_axis=0, concat_axis=0, tiled=True),
        lax.all_to_all(maxima, "ctx", split_axis=0, concat_axis=0, tiled=True),
        lax.all_to_all(totals, "ctx", split_axis=0, concat_axis=0, tiled=True),
    )
    maxima = maxima.reshape(sources, own_rows, heads_here)
    totals = totals.reshape(sources, own_rows, heads_here)
    weighted = weighted.reshape(sources, own_rows, heads_here, HD)
    row_top = jnp.max(maxima, axis=0)
    factors = jnp.exp(maxima - row_top[None])
    summed = jnp.sum(factors * totals, axis=0)
    merged = jnp.sum(weighted * factors[..., None], axis=0) / summed[..., None]
    attended = merged.reshape(own_rows, heads_here * HD).astype(jnp.bfloat16)
    partial_value = jnp.dot(attended, out_weight, preferred_element_type=jnp.float32)
    return lax.psum_scatter(partial_value, "head", scatter_dimension=1, tiled=True)


def solution(mesh):
    in_specs = (P("ctx", "head"), P("ctx", "head"), P("ctx", "head"), P("ctx"), P("head", None))
    out_specs = P("ctx", "head")
    return jax.shard_map(
        on_device, mesh=mesh, in_specs=in_specs, out_specs=out_specs, check_vma=False
    )
```

profile of v0, /device:TPU:0, one launch (start us, length us, event | category | flops | bytes accessed | tf_op | source)
XLA Modules:
  0.0 490.3 jit_solution(4327720682232113588)
XLA Ops:
  6.5 0.0 all-gather.2.cloned.1.call-start
  6.5 0.7 all-gather.2.cloned.1.call-update
  7.3 6.5 %copy.13 = bf16[2048,1024]{0,1:T(8,128)(2,1)} copy(bf16[2048,1024]{1,0:T(8,128)(2,1)} %param.10) | data formatting | bytes 8388608 | tf_op args[1]
  13.8 6.5 %copy.16 = bf16[2048,8,128]{2,0,1:T(8,128)(2,1)} copy(bf16[2048,8,128]{0,2,1:T(8,128)(2,1)} %bitcast.55) | data formatting | bytes 8388608
  20.3 0.0 copy-start
  20.3 0.0 copy-start.1
  20.3 0.0 copy-start.4
  20.4 0.0 copy-start.5
  20.4 0.0 copy-start.6
  20.4 6.6 %copy.14 = bf16[2048,1024]{0,1:T(8,128)(2,1)} copy(bf16[2048,1024]{1,0:T(8,128)(2,1)} %param.11) | data formatting | bytes 8388608 | tf_op args[2]
  27.0 0.0 copy-done.7
  27.0 0.7 fusion.17
  27.7 21.0 %all-gather.2.cloned.1.call-done = bf16[2048,1024]{1,0:T(8,128)(2,1)} async-done(((bf16[256,1024]{1,0:T(8,128)(2,1)}), bf16[2048,1024]{1,0:T(8,128)(2,1)}) %all-gather.2.cloned.1.call-update) | async-done | bytes 4194320 | tf_op jit(solution)/shard_map/all_gather | solution.py:13
  48.7 5.2 %copy.25 = bf16[256,8,8,128]{3,2,1,0:T(8,128)(2,1)} copy(bf16[256,8,8,128]{3,1,2,0:T(8,128)(2,1)} %bitcast.58) | data formatting | bytes 8388608
  53.9 0.0 copy-done
  53.9 0.0 copy-done.1
  53.9 0.0 copy-done.2
  53.9 0.0 copy-done.3
  53.9 0.0 copy-done.4
  53.9 0.0 copy-done.5
  54.0 0.0 copy-done.6
  54.0 223.6 %while.16 = (s32[]{:T(128)}, f32[4,512,1024]{2,1,0:T(8,128)}, f32[4,512,8]{1,2,0:T(8,128)S(1)}, f32[4,512,8]{1,2,0:T(8,128)S(1)}, bf16[4,512,8,128]{3,2,1,0:T(8,...) while((s32[]{:T(128)}, f32[4,512,1024]{2,1,0:T(8,128)}, ...), condition=%wide.region_3.4_spmd.clone, body=%wide.region_0.3_spmd.clone.sunk | while | flops 4387264512 | bytes 122862320 | solution.py:52
  54.0 4.8 fusion.31
  58.8 1.3 constant_dynamic-slice_fusion.2
  60.1 15.4 %fusion.32 = (f32[8,512]{1,0:T(8,128)S(1)}, f32[8,512,2048]{2,1,0:T(8,128)}) fusion(f32[2048]{0:T(1024)S(1)} %fusion.31, bf16[2048,8,128]{2,0,1:T(8,128)(2,1)} %get-tuple-element.328, bf16[1,512,8,128]{3,2,1,0:T(8,128)(2,1)S(1)} %constant_dynamic-slice_fusion.2), kind=kOutput, calls=%fused_computation.3.clone.1 | convolution fusion | flops 2172645376 | bytes 38821888 | tf_op jit(solution)/shard_map/while/body/eval_jaxpr/ihd,jhd->hij/dot_general | solution.py:30
  75.5 14.4 %fusion.34 = f32[8,512]{1,0:T(8,128)S(1)} fusion(f32[8,512,2048]{2,1,0:T(8,128)} %get-tuple-element.273, f32[8,512]{1,0:T(8,128)S(1)} %get-tuple-element.274, f32[2048]{0:T(1024)S(1)} %fusion.31), kind=kLoop, calls=%fused_computation.4.clone.1 | loop fusion | flops 33550336 | bytes 33595392 | tf_op jit(solution)/shard_map/while/body/eval_jaxpr/reduce_sum | solution.py:37
  89.9 16.6 %fusion.33 = f32[8,512,128]{1,2,0:T(8,128)} fusion(bf16[2048,8,128]{0,2,1:T(8,128)(2,1)} %get-tuple-element.329, f32[8,512,2048]{2,1,0:T(8,128)} %get-tuple-element.273, f32[8,512]{1,0:T(8,128)S(1)} %get-tuple-element.274, f32[2048]{0:T(1024)S(1)} %fusion.31), kind=kOutput, calls=%fused_computation.6.clone.1 | convolution fusion | flops 2181038080 | bytes 39870464 | tf_op jit(solution)/shard_map/while/body/eval_jaxpr/hij,jhd->ihd/dot_general | solution.py:38
  106.5 1.9 copy.36
  108.4 1.5 constant_dynamic-update-slice_fusion.2
  109.9 4.8 fusion.31
  114.7 1.3 constant_dynamic-slice_fusion.2
  116.0 15.4 %fusion.32 = (f32[8,512]{1,0:T(8,128)S(1)}, f32[8,512,2048]{2,1,0:T(8,128)}) fusion(f32[2048]{0:T(1024)S(1)} %fusion.31, bf16[2048,8,128]{2,0,1:T(8,128)(2,1)} %get-tuple-element.328, bf16[1,512,8,128]{3,2,1,0:T(8,128)(2,1)S(1)} %constant_dynamic-slice_fusion.2), kind=kOutput, calls=%fused_computation.3.clone.1 | convolution fusion | flops 2172645376 | bytes 38821888 | tf_op jit(solution)/shard_map/while/body/eval_jaxpr/ihd,jhd->hij/dot_general | solution.py:30
  131.4 14.4 %fusion.34 = f32[8,512]{1,0:T(8,128)S(1)} fusion(f32[8,512,2048]{2,1,0:T(8,128)} %get-tuple-element.273, f32[8,512]{1,0:T(8,128)S(1)} %get-tuple-element.274, f32[2048]{0:T(1024)S(1)} %fusion.31), kind=kLoop, calls=%fused_computation.4.clone.1 | loop fusion | flops 33550336 | bytes 33595392 | tf_op jit(solution)/shard_map/while/body/eval_jaxpr/reduce_sum | solution.py:37
  145.8 16.6 %fusion.33 = f32[8,512,128]{1,2,0:T(8,128)} fusion(bf16[2048,8,128]{0,2,1:T(8,128)(2,1)} %get-tuple-element.329, f32[8,512,2048]{2,1,0:T(8,128)} %get-tuple-element.273, f32[8,512]{1,0:T(8,128)S(1)} %get-tuple-element.274, f32[2048]{0:T(1024)S(1)} %fusion.31), kind=kOutput, calls=%fused_computation.6.clone.1 | convolution fusion | flops 2181038080 | bytes 39870464 | tf_op jit(solution)/shard_map/while/body/eval_jaxpr/hij,jhd->ihd/dot_general | solution.py:38
  162.4 1.9 copy.36
  164.3 1.5 constant_dynamic-update-slice_fusion.2
  165.8 4.8 fusion.31
  170.6 1.3 constant_dynamic-slice_fusion.2
  171.9 15.4 %fusion.32 = (f32[8,512]{1,0:T(8,128)S(1)}, f32[8,512,2048]{2,1,0:T(8,128)}) fusion(f32[2048]{0:T(1024)S(1)} %fusion.31, bf16[2048,8,128]{2,0,1:T(8,128)(2,1)} %get-tuple-element.328, bf16[1,512,8,128]{3,2,1,0:T(8,128)(2,1)S(1)} %constant_dynamic-slice_fusion.2), kind=kOutput, calls=%fused_computation.3.clone.1 | convolution fusion | flops 2172645376 | bytes 38821888 | tf_op jit(solution)/shard_map/while/body/eval_jaxpr/ihd,jhd->hij/dot_general | solution.py:30
  187.3 14.4 %fusion.34 = f32[8,512]{1,0:T(8,128)S(1)} fusion(f32[8,512,2048]{2,1,0:T(8,128)} %get-tuple-element.273, f32[8,512]{1,0:T(8,128)S(1)} %get-tuple-element.274, f32[2048]{0:T(1024)S(1)} %fusion.31), kind=kLoop, calls=%fused_computation.4.clone.1 | loop fusion | flops 33550336 | bytes 33595392 | tf_op jit(solution)/shard_map/while/body/eval_jaxpr/reduce_sum | solution.py:37
  201.8 16.5 %fusion.33 = f32[8,512,128]{1,2,0:T(8,128)} fusion(bf16[2048,8,128]{0,2,1:T(8,128)(2,1)} %get-tuple-element.329, f32[8,512,2048]{2,1,0:T(8,128)} %get-tuple-element.273, f32[8,512]{1,0:T(8,128)S(1)} %get-tuple-element.274, f32[2048]{0:T(1024)S(1)} %fusion.31), kind=kOutput, calls=%fused_computation.6.clone.1 | convolution fusion | flops 2181038080 | bytes 39870464 | tf_op jit(solution)/shard_map/while/body/eval_jaxpr/hij,jhd->ihd/dot_general | solution.py:38
  218.3 1.9 copy.36
  220.2 1.5 constant_dynamic-update-slice_fusion.2
  221.7 4.8 fusion.31
  226.5 1.3 constant_dynamic-slice_fusion.2
  227.8 15.4 %fusion.32 = (f32[8,512]{1,0:T(8,128)S(1)}, f32[8,512,2048]{2,1,0:T(8,128)}) fusion(f32[2048]{0:T(1024)S(1)} %fusion.31, bf16[2048,8,128]{2,0,1:T(8,128)(2,1)} %get-tuple-element.328, bf16[1,512,8,128]{3,2,1,0:T(8,128)(2,1)S(1)} %constant_dynamic-slice_fusion.2), kind=kOutput, calls=%fused_computation.3.clone.1 | convolution fusion | flops 2172645376 | bytes 38821888 | tf_op jit(solution)/shard_map/while/body/eval_jaxpr/ihd,jhd->hij/dot_general | solution.py:30
  243.2 14.4 %fusion.34 = f32[8,512]{1,0:T(8,128)S(1)} fusion(f32[8,512,2048]{2,1,0:T(8,128)} %get-tuple-element.273, f32[8,512]{1,0:T(8,128)S(1)} %get-tuple-element.274, f32[2048]{0:T(1024)S(1)} %fusion.31), kind=kLoop, calls=%fused_computation.4.clone.1 | loop fusion | flops 33550336 | bytes 33595392 | tf_op jit(solution)/shard_map/while/body/eval_jaxpr/reduce_sum | solution.py:37
  257.7 16.6 %fusion.33 = f32[8,512,128]{1,2,0:T(8,128)} fusion(bf16[2048,8,128]{0,2,1:T(8,128)(2,1)} %get-tuple-element.329, f32[8,512,2048]{2,1,0:T(8,128)} %get-tuple-element.273, f32[8,512]{1,0:T(8,128)S(1)} %get-tuple-element.274, f32[2048]{0:T(1024)S(1)} %fusion.31), kind=kOutput, calls=%fused_computation.6.clone.1 | convolution fusion | flops 2181038080 | bytes 39870464 | tf_op jit(solution)/shard_map/while/body/eval_jaxpr/hij,jhd->ihd/dot_general | solution.py:38
  274.2 1.9 copy.36
  276.1 1.5 constant_dynamic-update-slice_fusion.2
  277.6 7.6 %all_to_all.27 = f32[8,256,8]{1,2,0:T(8,128)S(1)} all-to-all(f32[8,256,8]{1,2,0:T(8,128)S(1)} %bitcast.60), channel_id=1, replica_groups=mesh['ctx'=8,'head'=4] {'ctx'}, dimensions={0} | all-to-all | bytes 131072 | tf_op jit(solution)/shard_map/all_to_all | solution.py:58
  285.2 7.4 %all_to_all.28 = f32[8,256,8]{1,2,0:T(8,128)S(1)} all-to-all(f32[8,256,8]{1,2,0:T(8,128)S(1)} %bitcast.61), channel_id=1, replica_groups=mesh['ctx'=8,'head'=4] {'ctx'}, dimensions={0} | all-to-all | bytes 131072 | tf_op jit(solution)/shard_map/all_to_all | solution.py:59
  292.5 4.9 %all-to-all-start = ((f32[8,256,1024]{2,1,0:T(8,128)}), f32[8,256,1024]{2,1,0:T(8,128)}, u32[]{:S(2)}, u32[]{:S(2)}) async-start(f32[8,256,1024]{2,1,0:T(8,128)} %bitcast.56), calls=%async_computation | async-start | bytes 16777216 | tf_op jit(solution)/shard_map/all_to_all | solution.py:57
  297.5 0.2 reduce-scatter.2.cloned.1.call-start
  297.8 0.3 copy.18
  298.1 4.5 mul.17
  302.6 9.3 %mul.18 = f32[8,256,1024]{2,1,0:T(8,128)} reshape(f32[8,256,8,128]{3,2,1,0:T(8,128)} %mul.17) | data formatting | bytes 16777216 | tf_op jit(solution)/shard_map/mul | solution.py:67
  311.9 0.1 copy.19
  312.0 79.5 %all-to-all-done = f32[8,256,1024]{2,1,0:T(8,128)} async-done(((f32[8,256,1024]{2,1,0:T(8,128)}), f32[8,256,1024]{2,1,0:T(8,128)}, u32[]{:S(2)}, u32[]{:S(2)}) %all-to-all-start) | async-done | bytes 8388640 | tf_op jit(solution)/shard_map/all_to_all | solution.py:57
  391.6 7.9 %multiply_reduce_fusion = f32[256,1024]{1,0:T(8,128)S(1)} fusion(f32[8,256,1024]{2,1,0:T(8,128)} %all-to-all-done, f32[8,256,1024]{2,1,0:T(8,128)} %mul.18), kind=kLoop, calls=%fused_computation.21 | loop fusion | flops 3932160 | bytes 17825792 | tf_op jit(solution)/shard_map/reduce_sum | solution.py:67
  399.4 0.3 div.11
  399.8 7.7 %fusion.15 = f32[256,4096]{1,0:T(8,128)} fusion(bf16[1024,4096]{1,0:T(8,128)(2,1)} %param.13, f32[256,1024]{1,0:T(8,128)S(1)} %multiply_reduce_fusion, f32[32,8,8,128]{3,2,1,0:T(8,128)S(1)} %bitcast.59), kind=kOutput, calls=%fused_computation.24 | convolution fusion | flops 2148007936 | bytes 14680064 | tf_op jit(solution)/shard_map/dot_general | solution.py:69
  407.4 0.0 reduce-scatter.2.cloned.1.call-update
  407.5 76.0 %reduce-scatter.2.cloned.1.call-done = f32[256,1024]{1,0:T(8,128)} async-done(((f32[256,4096]{1,0:T(8,128)}), f32[256,1024]{1,0:T(8,128)}) %reduce-scatter.2.cloned.1.call-update) | async-done | bytes 1048592 | tf_op jit(solution)/shard_map/reduce_scatter | solution.py:70
  (12 shorter events, 0.1 us)
Async XLA Ops:
  6.5 42.2 %all-gather.2.cloned.1.call-start = ((), (), s32[]{:S(2)}) async-start(), calls=%async_computation.4 | async-start | bytes 4718592 | tf_op jit(solution)/shard_map/all_gather | solution.py:13
  13.8 13.2 %copy-start.7 = (s32[8]{0:T(128)S(1)}, s32[8]{0:T(128)}, u32[]{:S(2)}) copy-start(s32[8]{0:T(128)} %param.12) | copy-start | bytes 100
  20.3 33.6 %copy-start = (pred[2048]{0:T(1024)(128)(4,1)S(1)}, pred[2048]{0:T(1024)(128)(4,1)}, u32[]{:S(2)}) copy-start(pred[2048]{0:T(1024)(128)(4,1)} %constant.199) | copy-start | bytes 6148
  20.3 33.6 %copy-start.1 = (pred[2048]{0:T(1024)(128)(4,1)S(1)}, pred[2048]{0:T(1024)(128)(4,1)}, u32[]{:S(2)}) copy-start(pred[2048]{0:T(1024)(128)(4,1)} %constant.200) | copy-start | bytes 6148
  20.3 33.6 %copy-start.2 = (pred[2048]{0:T(1024)(128)(4,1)S(1)}, pred[2048]{0:T(1024)(128)(4,1)}, u32[]{:S(2)}) copy-start(pred[2048]{0:T(1024)(128)(4,1)} %constant.201) | copy-start | bytes 6148
  20.3 33.6 %copy-start.3 = (pred[2048]{0:T(1024)(128)(4,1)S(1)}, pred[2048]{0:T(1024)(128)(4,1)}, u32[]{:S(2)}) copy-start(pred[2048]{0:T(1024)(128)(4,1)} %constant.202) | copy-start | bytes 6148
  20.3 33.6 %copy-start.4 = (pred[2048]{0:T(1024)(128)(4,1)S(1)}, pred[2048]{0:T(1024)(128)(4,1)}, u32[]{:S(2)}) copy-start(pred[2048]{0:T(1024)(128)(4,1)} %constant.203) | copy-start | bytes 6148
  20.4 33.6 %copy-start.5 = (pred[2048]{0:T(1024)(128)(4,1)S(1)}, pred[2048]{0:T(1024)(128)(4,1)}, u32[]{:S(2)}) copy-start(pred[2048]{0:T(1024)(128)(4,1)} %constant.204) | copy-start | bytes 6148
  20.4 33.6 %copy-start.6 = (pred[2048]{0:T(1024)(128)(4,1)S(1)}, pred[2048]{0:T(1024)(128)(4,1)}, u32[]{:S(2)}) copy-start(pred[2048]{0:T(1024)(128)(4,1)} %constant.205) | copy-start | bytes 6148
  292.5 99.0 %all-to-all-start = ((f32[8,256,1024]{2,1,0:T(8,128)}), f32[8,256,1024]{2,1,0:T(8,128)}, u32[]{:S(2)}, u32[]{:S(2)}) async-start(f32[8,256,1024]{2,1,0:T(8,128)} %bitcast.56), calls=%async_computation | async-start | bytes 16777216 | tf_op jit(solution)/shard_map/all_to_all | solution.py:57
  297.5 186.0 %reduce-scatter.2.cloned.1.call-start = ((), (), s32[]{:S(2)}) async-start(), calls=%async_computation.5 | async-start | bytes 5242880 | tf_op jit(solution)/shard_map/reduce_scatter | solution.py:70
Sparse Core Ops, SparseCore 0:
  9.2 39.4 all-gather.1
  407.6 75.8 reduce-scatter.1
where the time goes:
time: 492 us; the launch traced here: 490 us
  waiting for transfers between devices  177 us (36%)
  matrix products  136 us (28%)
  other arithmetic  84.8 us (17%)
  local copies, waits for them, and re-layouts  58.9 us (12%)
  blocking collectives  14.9 us (3%)
  between operations  13.5 us (3%)
  starting transfers between devices  5.16 us (1%)
    all_to_all x1, waiting for transfers between devices, on_device(): lax.all_to_all(weighted, 'ctx', split_axis=0, concat_axis=0, tiled=True)  79.5 us
    reduce_scatter x1, waiting for transfers between devices, on_device(): lax.psum_scatter(partial_value, 'head', scatter_dimension=1, tiled=True)  76 us
    dot_general x4, matrix products, weigh(): jnp.einsum('hij,jhd->ihd', raised.astype(jnp.bfloat16), value_heads, pref...  66.2 us
    dot_general x4, matrix products, scores_of(): jnp.einsum('ihd,jhd->hij', query_rows, key_heads, preferred_element_type=...  61.6 us
    reduce_sum x4, other arithmetic, weigh(): totals = jnp.sum(raised, axis=2)  57.7 us
    unnamed x20, local copies, waits for them, and re-layouts  24.9 us
    all_gather x1, waiting for transfers between devices, on_device(): whole = lax.all_gather(queries, 'ctx', axis=0, tiled=True)  21 us
    select_n x4, other arithmetic, on_device(): jnp.where(positions % SPAN < limits, 0.0, -1e+30).astype(jnp.float32)  19.1 us
  transfers between devices with their start and end apart: 3, of which 3 were waited for; matrix products, arithmetic and copies ran while one was open for 7% of the time, Pallas kernels for 0%

commit v1 on v0

v1 whole, which is shorter than its diff:
```python
import functools
import math

import jax
import jax.numpy as jnp
from jax import lax
from jax.experimental import pallas as pl
from jax.experimental.pallas import tpu as pltpu
from jax.sharding import PartitionSpec as P

HD = 128
SPAN = 256
STEP = 16
BLOCK = 512
SUB = 256
CHUNKS = 2
STATS = 16
SCALE = math.log2(math.e) / math.sqrt(HD)
NT = (((1,), (1,)), ((), ()))
NN = (((1,), (0,)), ((), ()))
MIB = 2**20


def compact_kernel(spans, meta, own_k, own_v, got_k, got_v, out_k, out_v, out_m):
    head = pl.program_id(0)
    rows = lax.broadcasted_iota(jnp.int32, (SPAN, HD), 0)
    here = own_k.shape[0] // SPAN
    at = jnp.int32(0)
    for passage in range(2 * here):
        source_k, source_v = (own_k, own_v) if passage < here else (got_k, got_v)
        part = pl.ds((passage % here) * SPAN, SPAN)
        size = spans[passage]
        valid = rows < size
        k = source_k[part, :].astype(jnp.float32)
        v = source_v[part, :].astype(jnp.float32)
        first = jnp.broadcast_to(k[:1, :], k.shape)
        place = pl.ds(pl.multiple_of(at, STEP), SPAN)
        out_k[place, :] = jnp.where(valid, k, first).astype(jnp.bfloat16)
        out_v[place, :] = jnp.where(valid, v, 0.0).astype(jnp.bfloat16)

        @pl.when(head == 0)
        def _():
            out_m[place, :] = jnp.where(valid, 1.0, 0.0).astype(jnp.bfloat16)

        at = at + (size + STEP - 1) // STEP * STEP
    for extra in range(BLOCK // SPAN):
        place = pl.ds(pl.multiple_of(at + extra * SPAN, STEP), SPAN)
        out_k[place, :] = first.astype(jnp.bfloat16)
        out_v[place, :] = jnp.zeros((SPAN, HD), jnp.bfloat16)

        @pl.when(head == 0)
        def _():
            out_m[place, :] = jnp.zeros((SPAN, HD), jnp.bfloat16)


def compact(spans, core, keys, values, got_k, got_v):
    tokens, width = got_k.shape
    heads = width // HD
    size = 2 * tokens + BLOCK
    own = pl.BlockSpec((tokens, HD), lambda h, s, m: (0, m[0] * heads + h))
    got = pl.BlockSpec((tokens, HD), lambda h, s, m: (0, h))
    out = pl.BlockSpec((size, HD), lambda h, s, m: (0, h))
    return pl.pallas_call(
        compact_kernel,
        grid_spec=pltpu.PrefetchScalarGridSpec(
            num_scalar_prefetch=2,
            grid=(heads,),
            in_specs=[own, own, got, got],
            out_specs=[out, out, pl.BlockSpec((size, HD), lambda h, s, m: (0, 0))],
        ),
        out_shape=[
            jax.ShapeDtypeStruct((size, width), jnp.bfloat16),
            jax.ShapeDtypeStruct((size, width), jnp.bfloat16),
            jax.ShapeDtypeStruct((size, HD), jnp.bfloat16),
        ],
        compiler_params=pltpu.CompilerParams(vmem_limit_bytes=40 * MIB),
        cost_estimate=pl.CostEstimate(
            flops=0, bytes_accessed=8 * width * size, transcendentals=0
        ),
        name="compact",
    )(spans, core, keys, values, got_k, got_v)


def attend_kernel(blocks, tiles, count, *refs):
    q_refs, (k_ref, v_ref, m_ref) = refs[:blocks], refs[blocks : blocks + 3]
    o_refs = refs[blocks + 3 : 2 * blocks + 3]
    q_all, s_even, s_odd, top_even, top_odd, acc = refs[2 * blocks + 3 :]
    rows = q_refs[0].shape[0]
    step = pl.program_id(0)
    turns = (count[0] + BLOCK - 1) // BLOCK
    total = blocks * rows
    sub = min(SUB, total)

    def score(at, scores, top, part):
        s = lax.dot_general(
            q_all[part, :], k_ref[at, :], NT, preferred_element_type=jnp.float32
        )
        scores[part, at] = s
        most = top[part, :]
        for i in range(BLOCK // HD):
            most = jnp.maximum(most, s[:, i * HD : (i + 1) * HD])
        top[part, :] = most

    def weigh(at, scores, top, part):
        value = jnp.concatenate([v_ref[at, :], m_ref[at, :]], axis=1)
        most = top[part, :]
        s = scores[part, at]
        weights = jnp.concatenate(
            [
                jnp.exp2((s[:, i * HD : (i + 1) * HD] - most) * SCALE).astype(jnp.bfloat16)
                for i in range(BLOCK // HD)
            ],
            axis=1,
        )
        acc[part, :] += lax.dot_general(
            weights, value, NN, preferred_element_type=jnp.float32
        )

    def run(now, then):
        if then is not None:
            scores_then, top_then = then
            top_then[...] = jnp.broadcast_to(
                jnp.max(top_then[...], axis=1, keepdims=True), top_then.shape
            )
            acc[...] = jnp.zeros_like(acc)
        if now is not None:
            scores_now, top_now = now
            top_now[...] = jnp.full(top_now.shape, -3e38, jnp.float32)
            for b in range(blocks):
                q_all[b * rows : (b + 1) * rows, :] = q_refs[b][...]

        def body(turn, carry):
            at = pl.ds(pl.multiple_of(turn * BLOCK, BLOCK), BLOCK)
            for r in range(total // sub):
                part = pl.ds(r * sub, sub)
                if now is not None:
                    score(at, scores_now, top_now, part)
                if then is not None:
                    weigh(at, scores_then, top_then, part)
            return carry

        lax.fori_loop(0, turns, body, 0)
        if then is not None:
            for b in range(blocks):
                finish(b, top_then)

    def finish(b, top):
        group = min(rows, HD)
        for u in range(rows // group):
            part = pl.ds(b * rows + u * group, group)
            sums = acc[part, HD:]
            o_refs[b][u * group : (u + 1) * group, :] = (acc[part, :HD] / sums).astype(
                jnp.bfloat16
            )
            logs = top[part, :] * SCALE + jnp.log2(sums)
            eye = lax.broadcasted_iota(jnp.int32, (group, HD), 0) == (
                lax.broadcasted_iota(jnp.int32, (group, HD), 1)
            )
            line = jnp.sum(jnp.where(eye, logs, 0.0), axis=0, keepdims=True)
            high = line.astype(jnp.bfloat16).astype(jnp.float32)
            middle = (line - high).astype(jnp.bfloat16).astype(jnp.float32)
            low = line - high - middle
            index = lax.broadcasted_iota(jnp.int32, (STATS, HD), 0)
            packed = jnp.where(
                index == 0,
                high,
                jnp.where(index == 1, middle, jnp.where(index == 2, low, 0.0)),
            )
            o_refs[b][rows + u * STATS : rows + (u + 1) * STATS, :] = packed.astype(
                jnp.bfloat16
            )

    even, odd = (s_even, top_even), (s_odd, top_odd)
    is_even = lax.rem(step, 2) == 0
    inside = jnp.logical_and(step > 0, step < tiles)

    @pl.when(step == 0)
    def _():
        run(even, None)

    if tiles > 1:

        @pl.when(jnp.logical_and(inside, is_even))
        def _():
            run(even, odd)

        @pl.when(jnp.logical_and(inside, jnp.logical_not(is_even)))
        def _():
            run(odd, even)

    @pl.when(step == tiles)
    def _():
        run(None, odd if tiles % 2 == 0 else even)


def stat_rows(rows):
    return STATS * (rows // min(rows, HD))


def attend(count, queries, chunk, key, value, mark):
    blocks = len(queries)
    rows = queries[0].shape[0] // CHUNKS
    width = queries[0].shape[1]
    heads = width // HD
    size = key.shape[0]
    tall = rows + stat_rows(rows)
    now = lambda t: jnp.minimum(t, heads - 1)
    then = lambda t: jnp.maximum(t - 1, 0)
    total = blocks * rows
    return pl.pallas_call(
        functools.partial(attend_kernel, blocks, heads),
        grid_spec=pltpu.PrefetchScalarGridSpec(
            num_scalar_prefetch=1,
            grid=(heads + 1,),
            in_specs=[pl.BlockSpec((rows, HD), lambda t, n: (chunk, now(t)))] * blocks
            + [
                pl.BlockSpec((size, HD), lambda t, n: (0, now(t))),
                pl.BlockSpec((size, HD), lambda t, n: (0, then(t))),
                pl.BlockSpec((size, HD), lambda t, n: (0, 0)),
            ],
            out_specs=[pl.BlockSpec((tall, HD), lambda t, n: (0, then(t)))] * blocks,
            scratch_shapes=[
                pltpu.VMEM((total, HD), jnp.bfloat16),
                pltpu.VMEM((total, size), jnp.float32),
                pltpu.VMEM((total, size), jnp.float32),
                pltpu.VMEM((total, HD), jnp.float32),
                pltpu.VMEM((total, HD), jnp.float32),
                pltpu.VMEM((total, 2 * HD), jnp.float32),
            ],
        ),
        out_shape=[jax.ShapeDtypeStruct((tall, width), jnp.bfloat16)] * blocks,
        compiler_params=pltpu.CompilerParams(vmem_limit_bytes=58 * MIB),
        cost_estimate=pl.CostEstimate(
            flops=8 * total * size * width // 2, bytes_accessed=4 * size * width, transcendentals=0
        ),
        name="attend",
    )(count, *queries, key, value, mark)


def project_kernel(sources, order, meta, *refs):
    parts, weight = refs[: 2 * sources], refs[2 * sources]
    outs, attended = refs[2 * sources + 1 : -1], refs[-1]
    step = pl.program_id(0)
    rows = outs[0].shape[0]
    width = parts[0].shape[1]
    group = min(rows, HD)

    @pl.when(step == 0)
    def _():
        eye = lax.broadcasted_iota(jnp.int32, (group, HD), 0) == (
            lax.broadcasted_iota(jnp.int32, (group, HD), 1)
        )
        for side in range(2):
            mine = parts[side * sources : (side + 1) * sources]
            core = meta[0] if side == 0 else 1 - meta[0]
            for u in range(rows // group):
                there = slice(u * group, (u + 1) * group)
                for head in range(width // HD):
                    cols = slice(head * HD, (head + 1) * HD)
                    logs = []
                    for part in mine:
                        stats = part[rows + u * STATS : rows + (u + 1) * STATS, cols]
                        stats = stats.astype(jnp.float32)
                        logs.append(stats[0:1] + (stats[1:2] + stats[2:3]))
                    most = functools.reduce(jnp.maximum, logs)
                    shares = [jnp.exp2(x - most) for x in logs]
                    whole = functools.reduce(jnp.add, shares)
                    merged = None
                    for part, share in zip(mine, shares):
                        line = jnp.broadcast_to(share / whole, (group, HD))
                        column = jnp.sum(jnp.where(eye, line, 0.0), axis=1, keepdims=True)
                        term = part[there, cols].astype(jnp.float32) * column
                        merged = term if merged is None else merged + term
                    place = pl.ds(pl.multiple_of(core * width + head * HD, HD), HD)
                    attended[there, place] = merged.astype(jnp.bfloat16)

    for i in range(len(outs)):

        @pl.when(step == i)
        def _(i=i):
            outs[i][...] = lax.dot_general(
                attended[...], weight[...], NN, preferred_element_type=jnp.float32
            ).astype(outs[i].dtype)


def project(meta, own, other, out_weight, groups, rows):
    depth, total = out_weight.shape
    cols = total // groups
    sources = len(own)
    whole = pl.BlockSpec(own[0].shape, lambda t, m: (0, 0))
    order = [d for d in range(groups - 1, 0, -1)] + [0]
    return pl.pallas_call(
        functools.partial(project_kernel, sources, order),
        grid_spec=pltpu.PrefetchScalarGridSpec(
            num_scalar_prefetch=1,
            grid=(groups,),
            in_specs=[whole] * (2 * sources)
            + [pl.BlockSpec((depth, cols), lambda t, m: (0, m[1] ^ (groups - 1 - t)))],
            out_specs=[pl.BlockSpec((rows, cols), lambda t, m: (0, 0))] * groups,
            scratch_shapes=[pltpu.VMEM((rows, depth), jnp.bfloat16)],
        ),
        out_shape=[
            jax.ShapeDtypeStruct((rows, cols), jnp.bfloat16 if d else jnp.float32)
            for d in order
        ],
        compiler_params=pltpu.CompilerParams(vmem_limit_bytes=40 * MIB),
        cost_estimate=pl.CostEstimate(
            flops=2 * rows * depth * total, bytes_accessed=2 * depth * total, transcendentals=0
        ),
        name="project",
    )(meta, *own, *other, out_weight)


def on_device(queries, keys, values, lengths, out_weight):
    sources = lax.axis_size("ctx")
    groups = lax.axis_size("head")
    core = lax.rem(lax.axis_index("ctx"), 2)
    width = keys.shape[1] // 2
    meta = jnp.stack([core, lax.axis_index("head")]).astype(jnp.int32)

    def swap(x, k, axis="ctx"):
        n = sources if axis == "ctx" else groups
        return lax.ppermute(x, axis, [(i, i ^ k) for i in range(n)])

    def half(x, which):
        return lax.dynamic_slice(x, (0, which * width), (x.shape[0], width))

    got_k = swap(half(keys, 1 - core), 1)
    got_v = swap(half(values, 1 - core), 1)
    spans = jnp.concatenate([lengths, swap(lengths, 1)])
    count = jnp.sum((spans + STEP - 1) // STEP * STEP).reshape(1)
    mine, others = half(queries, core), half(queries, 1 - core)
    asked = [mine] + [swap(mine if k % 2 == 0 else others, k) for k in range(1, sources)]
    key, value, mark = compact(spans, meta, keys, values, got_k, got_v)

    rows = queries.shape[0] // CHUNKS
    outs = []
    for chunk in range(CHUNKS):
        partial = attend(count, asked, chunk, key, value, mark)
        back = [partial[0]] + [swap(partial[k], k) for k in range(1, sources)]
        blocks = project(meta, back[0::2], back[1::2], out_weight, groups, rows)
        total = blocks[-1]
        for d in range(groups - 1, 0, -1):
            total = total + swap(blocks[groups - 1 - d], d, "head").astype(jnp.float32)
        outs.append(total)
    return jnp.concatenate(outs, axis=0)


def solution(mesh):
    in_specs = (P("ctx", "head"), P("ctx", "head"), P("ctx", "head"), P("ctx"), P("head", None))
    out_specs = P("ctx", "head")
    return jax.shard_map(
        on_device, mesh=mesh, in_specs=in_specs, out_specs=out_specs, check_vma=False
    )
```

time: 492 us -> 154 us (0.31)
  matrix products: 136 us -> 0 us
  waiting for transfers between devices: 177 us -> 42.6 us
  other arithmetic: 84.8 us -> 2.23 us
  Pallas kernels: 0 us -> 58.2 us
  local copies, waits for them, and re-layouts: 58.9 us -> 17.1 us
  starting transfers between devices: 5.16 us -> 34.4 us
  blocking collectives: 14.9 us -> 0 us
  between operations: 13.5 us -> 0.16 us
    dot_general x9 -> x0, matrix products: 136 us -> none  [the longest x4 66.2 us: weigh(): jnp.einsum('hij,jhd->ihd', raised.astype(jnp.bfloat16), value_heads, pref...]
    all_to_all x1 -> x0, waiting for transfers between devices: 79.5 us -> none  [on_device(): lax.all_to_all(weighted, 'ctx', split_axis=0, concat_axis=0, tiled=True)]
    reduce_scatter x1 -> x0, waiting for transfers between devices: 76 us -> none  [on_device(): lax.psum_scatter(partial_value, 'head', scatter_dimension=1, tiled=True)]
    reduce_sum x6 -> x1, other arithmetic: 65.6 us -> 0.79 us  [on_device(): count = jnp.sum((spans + STEP - 1) // STEP * STEP).reshape(1)]
    pallas_call x0 -> x5, Pallas kernels: none -> 58.2 us  [the longest x2 42.7 us: attend(): pl.pallas_call(functools.partial(attend_kernel, blocks, heads), grid_spec...]
    ppermute x0 -> x30, waiting for transfers between devices: none -> 42.6 us  [swap(): return lax.ppermute(x, axis, [(i, i ^ k) for i in range(n)])]
    ppermute x0 -> x30, starting transfers between devices: none -> 34.4 us  [swap(): return lax.ppermute(x, axis, [(i, i ^ k) for i in range(n)])]
    all_gather x1 -> x0, waiting for transfers between devices: 21 us -> none  [on_device(): whole = lax.all_gather(queries, 'ctx', axis=0, tiled=True)]
  transfers between devices with their start and end apart: 3 -> 30, of which waited for: 3 -> 8; matrix products, arithmetic and copies ran while one was open for 7% -> 2% of each run, Pallas kernels for 0% -> 24%
where the time goes in v1:
time: 154 us; the launch traced here: 155 us
  Pallas kernels  58.2 us (38%)
  waiting for transfers between devices  42.6 us (28%)
  starting transfers between devices  34.4 us (22%)
  local copies, waits for them, and re-layouts  17.1 us (11%)
  other arithmetic  2.23 us (1%)
    pallas_call x2, Pallas kernels, attend(): pl.pallas_call(functools.partial(attend_kernel, blocks, heads), grid_spec...  42.7 us
    ppermute x30, waiting for transfers between devices, swap(): return lax.ppermute(x, axis, [(i, i ^ k) for i in range(n)])  42.6 us
    ppermute x30, starting transfers between devices, swap(): return lax.ppermute(x, axis, [(i, i ^ k) for i in range(n)])  34.4 us
    unnamed x30, local copies, waits for them, and re-layouts  12.2 us
    pallas_call x1, Pallas kernels, compact(): pl.pallas_call(compact_kernel, grid_spec=pltpu.PrefetchScalarGridSpec(num...  8.01 us
    pallas_call x2, Pallas kernels, project(): pl.pallas_call(functools.partial(project_kernel, sources, order), grid_sp...  7.54 us
    dynamic_slice x3, local copies, waits for them, and re-layouts, half(): return lax.dynamic_slice(x, (0, which * width), (x.shape[0], width))  4.86 us
  transfers between devices with their start and end apart: 30, of which 8 were waited for; matrix products, arithmetic and copies ran while one was open for 2% of the time, Pallas kernels for 24%

profile of v1, /device:TPU:0, one launch (start us, length us, event | category | flops | bytes accessed | tf_op | source)
XLA Modules:
  0.0 154.8 jit_solution(1798479954917634280)
XLA Ops:
  0.0 3.3 %constant_dynamic-slice_fusion.1 = bf16[2048,512]{1,0:T(8,128)(2,1)} fusion(bf16[2048,1024]{1,0:T(8,128)(2,1)} %own_k.1, s32[]{:T(128)S(6)} %select_n.15), kind=kLoop, calls=%fused_computation.8 | loop fusion | bytes 4194308 | tf_op jit(solution)/shard_map/dynamic_slice | solution.py:326
  3.3 0.5 collective-permute-start.8
  3.7 1.6 %constant_dynamic-slice_fusion = bf16[2048,512]{1,0:T(8,128)(2,1)} fusion(bf16[2048,1024]{1,0:T(8,128)(2,1)S(1)} %copy-done.3, s32[]{:T(128)S(6)} %select_n.15), kind=kLoop, calls=%fused_computation.7 | loop fusion | bytes 4194308 | tf_op jit(solution)/shard_map/dynamic_slice | solution.py:326
  5.3 0.0 collective-permute-start.9
  5.4 0.0 copy-start.9
  5.4 0.5 collective-permute-start.1
  5.9 2.6 %collective-permute-start.2 = (bf16[256,512]{1,0:T(8,128)(2,1)S(1)}, bf16[256,512]{1,0:T(8,128)(2,1)S(1)}, u32[]{:S(2)}, u32[]{:S(2)}) collective-permute-start(bf16[256,512]{1,0:T(8,128)(2,1)S(1)} %get-tuple-element.62.refs_0_), channel_id=1, source_target_pairs={{0,8},{4,12},{8,0},{12,4},{16,24},{20,28},{24,16},{28,20},{1,9},{5... | collective-permute-start | bytes 786440 | tf_op jit(solution)/shard_map/ppermute | solution.py:323
  8.5 0.2 collective-permute-start
  8.7 2.2 %collective-permute-done = s32[8]{0:T(128)S(1)} collective-permute-done((s32[8]{0:T(128)S(1)}, s32[8]{0:T(128)S(1)}, u32[]{:S(2)}, u32[]{:S(2)}) %collective-permute-start) | collective-permute-done | bytes 64 | tf_op jit(solution)/shard_map/ppermute | solution.py:323
  10.9 2.9 %collective-permute-start.4 = (bf16[256,512]{1,0:T(8,128)(2,1)S(1)}, bf16[256,512]{1,0:T(8,128)(2,1)}, u32[]{:S(2)}, u32[]{:S(2)}) collective-permute-start(bf16[256,512]{1,0:T(8,128)(2,1)S(1)} %get-tuple-element.62.refs_0_), channel_id=1, source_target_pairs={{0,16},{4,20},{8,24},{12,28},{16,0},{20,4},{24,8},{28,12},{1,17},{... | collective-permute-start | bytes 786440 | tf_op jit(solution)/shard_map/ppermute | solution.py:323
  13.8 1.8 %collective-permute-done.2.refs_2_ = bf16[256,512]{1,0:T(8,128)(2,1)S(1)} collective-permute-done((bf16[256,512]{1,0:T(8,128)(2,1)S(1)}, bf16[256,512]{1,0:T(8,128)(2,1)S(1)}, u32[]{:S(2)}, u32[]{:S(2)}) %collective-permute-start.2) | collective-permute-done | bytes 262176 | tf_op jit(solution)/shard_map/ppermute | solution.py:323
  15.7 0.8 collective-permute-start.5
  16.4 0.0 collective-permute-done.8.got_k
  16.5 2.2 %collective-permute-start.6 = (bf16[256,512]{1,0:T(8,128)(2,1)S(1)}, bf16[256,512]{1,0:T(8,128)(2,1)}, u32[]{:S(2)}, u32[]{:S(2)}) collective-permute-start(bf16[256,512]{1,0:T(8,128)(2,1)S(1)} %get-tuple-element.62.refs_0_), channel_id=1, source_target_pairs={{0,24},{4,28},{8,16},{12,20},{16,8},{20,12},{24,0},{28,4},{1,25},{... | collective-permute-start | bytes 786440 | tf_op jit(solution)/shard_map/ppermute | solution.py:323
  18.6 0.0 collective-permute-done.9.got_v
  18.6 1.3 collective-permute-start.7
  19.9 0.1 pad_add_fusion.meta
  20.0 0.8 multiply_reduce_fusion
  20.8 2.2 %copy-done.2 = bf16[2048,1024]{1,0:T(8,128)(2,1)S(1)} copy-done((bf16[2048,1024]{1,0:T(8,128)(2,1)S(1)}, bf16[2048,1024]{1,0:T(8,128)(2,1)}, u32[]{:S(2)}) %copy-start.2) | copy-done | bytes 4194328
  23.0 2.2 %copy-done.4 = bf16[2048,1024]{1,0:T(8,128)(2,1)S(1)} copy-done((bf16[2048,1024]{1,0:T(8,128)(2,1)S(1)}, bf16[2048,1024]{1,0:T(8,128)(2,1)}, u32[]{:S(2)}) %copy-start.4) | copy-done | bytes 4194328
  25.2 8.0 %compact.1 = (bf16[4608,512]{1,0:T(8,128)(2,1)}, bf16[4608,512]{1,0:T(8,128)(2,1)}, bf16[4608,128]{1,0:T(8,128)(2,1)S(1)}) custom-call(s32[16]{0:T(128)S(1)} %get-tuple-element.60.spans, s32[2]{0:T(128)S(1)} %pad_add_fusion.meta, bf16[2048,1024]{1,0:T(8,128)(2,1)S(1)} %copy-done.2, bf16[2048,1024]{1,0:T(8,128)(2,1)S(1)} %copy-done.4, ...), custom_call_target="tpu_custom_call" | custom-call | bytes 18874368 | tf_op jit(solution)/shard_map/compact/pallas_call | solution.py:63
  33.2 1.1 copy-done.7
  34.3 2.7 %collective-permute-done.5.refs_5_ = bf16[256,512]{1,0:T(8,128)(2,1)} collective-permute-done((bf16[256,512]{1,0:T(8,128)(2,1)S(1)}, bf16[256,512]{1,0:T(8,128)(2,1)}, u32[]{:S(2)}, u32[]{:S(2)}) %collective-permute-start.5) | collective-permute-done | bytes 262176 | tf_op jit(solution)/shard_map/ppermute | solution.py:323
  37.0 0.0 collective-permute-done.6.refs_6_
  37.0 0.0 collective-permute-done.7.refs_7_
  37.0 21.3 %attend.2 = (bf16[144,512]{1,0:T(8,128)(2,1)}, bf16[144,512]{1,0:T(8,128)(2,1)}, bf16[144,512]{1,0:T(8,128)(2,1)}, bf16[144,512]{1,0:T(8,128)(2,1)}, bf16[144,51...) custom-call(s32[1]{0:T(128)} %bitcast.2.count, ...), custom_call_target="tpu_custom_call" | custom-call | flops 9663676416 | bytes 9437184 | tf_op jit(solution)/shard_map/attend/pallas_call | solution.py:210
  58.3 2.2 %collective-permute-start.10 = (bf16[144,512]{1,0:T(8,128)(2,1)}, bf16[144,512]{1,0:T(8,128)(2,1)S(1)}, u32[]{:S(2)}, u32[]{:S(2)}) collective-permute-start(bf16[144,512]{1,0:T(8,128)(2,1)} %get-tuple-element.36), channel_id=1, source_target_pairs={{0,8},{4,12},{8,0},{12,4},{16,24},{20,28},{24,16},{28,20},{1,9},{5... | collective-permute-start | bytes 442376 | tf_op jit(solution)/shard_map/ppermute | solution.py:323
  60.5 1.3 collective-permute-start.11
  61.8 0.2 collective-permute-start.12
  62.0 2.1 %collective-permute-start.14 = (bf16[144,512]{1,0:T(8,128)(2,1)}, bf16[144,512]{1,0:T(8,128)(2,1)S(1)}, u32[]{:S(2)}, u32[]{:S(2)}) collective-permute-start(bf16[144,512]{1,0:T(8,128)(2,1)} %get-tuple-element.40), channel_id=1, source_target_pairs={{0,12},{4,8},{8,4},{12,0},{16,28},{20,24},{24,20},{28,16},{1,13},{... | collective-permute-start | bytes 442376 | tf_op jit(solution)/shard_map/ppermute | solution.py:323
  64.1 1.1 collective-permute-done.10.refs_1_
  65.2 0.9 collective-permute-start.15
  66.1 3.5 %collective-permute-done.11.refs_2_ = bf16[144,512]{1,0:T(8,128)(2,1)S(1)} collective-permute-done((bf16[144,512]{1,0:T(8,128)(2,1)}, bf16[144,512]{1,0:T(8,128)(2,1)S(1)}, u32[]{:S(2)}, u32[]{:S(2)}) %collective-permute-start.11) | collective-permute-done | bytes 147488 | tf_op jit(solution)/shard_map/ppermute | solution.py:323
  69.5 21.3 %attend.3 = (bf16[144,512]{1,0:T(8,128)(2,1)}, bf16[144,512]{1,0:T(8,128)(2,1)}, bf16[144,512]{1,0:T(8,128)(2,1)}, bf16[144,512]{1,0:T(8,128)(2,1)}, bf16[144,51...) custom-call(s32[1]{0:T(128)} %bitcast.2.count, ...), custom_call_target="tpu_custom_call" | custom-call | flops 9663676416 | bytes 9437184 | tf_op jit(solution)/shard_map/attend/pallas_call | solution.py:210
  90.9 0.0 collective-permute-done.12.refs_3_
  90.9 2.1 %collective-permute-start.20 = (bf16[144,512]{1,0:T(8,128)(2,1)}, bf16[144,512]{1,0:T(8,128)(2,1)S(1)}, u32[]{:S(2)}, u32[]{:S(2)}) collective-permute-start(bf16[144,512]{1,0:T(8,128)(2,1)} %get-tuple-element.48), channel_id=1, source_target_pairs={{0,8},{4,12},{8,0},{12,4},{16,24},{20,28},{24,16},{28,20},{1,9},{5... | collective-permute-start | bytes 442376 | tf_op jit(solution)/shard_map/ppermute | solution.py:323
  93.0 1.5 collective-permute-start.22
  94.6 1.3 collective-permute-start.23
  95.9 0.0 collective-permute-done.16.refs_7_
  95.9 1.3 collective-permute-start.24
  97.3 3.4 %copy-done = bf16[1024,4096]{1,0:T(8,128)(2,1)S(1)} copy-done((bf16[1024,4096]{1,0:T(8,128)(2,1)S(1)}, bf16[1024,4096]{1,0:T(8,128)(2,1)}, u32[]{:S(2)}) %copy-start) | copy-done | bytes 8388632
  100.6 3.7 %project.2 = (bf16[128,1024]{1,0:T(8,128)(2,1)S(1)}, bf16[128,1024]{1,0:T(8,128)(2,1)S(1)}, bf16[128,1024]{1,0:T(8,128)(2,1)S(1)}, f32[128,1024]{1,0:T(8,128)S(1)}) custom-call(s32[2]{0:T(128)S(1)} %pad_add_fusion.meta, bf16[144,512]{1,0:T(8,128)(2,1)S(1)} %copy-done.6, bf16[144,512]{1,0:T(8,128)(2,1)S(1)} %collective-permute-done.10.refs_1_, ...), custom_call_target="tpu_custom_call" | custom-call | flops 1073741824 | bytes 8388608 | tf_op jit(solution)/shard_map/project/pallas_call | solution.py:292
  104.3 0.0 collective-permute-done.20.refs_1_
  104.3 3.7 %collective-permute-start.17 = (bf16[128,1024]{1,0:T(8,128)(2,1)S(1)}, bf16[128,1024]{1,0:T(8,128)(2,1)S(1)}, u32[]{:S(2)}, u32[]{:S(2)}) collective-permute-start(bf16[128,1024]{1,0:T(8,128)(2,1)S(1)} %get-tuple-element.44), channel_id=1, source_target_pairs={{0,3},{1,2},{2,1},{3,0},{4,7},{5,6},{6,5},{7,4},{8,11},{9,10},{10,... | collective-permute-start | bytes 786440 | tf_op jit(solution)/shard_map/ppermute | solution.py:323
  108.1 0.0 collective-permute-done.21.refs_2_
  108.1 0.0 collective-permute-start.18
  108.1 0.0 collective-permute-done.22.refs_3_
  108.1 0.7 collective-permute-start.19
  108.8 0.0 collective-permute-done.23.refs_4_
  108.8 0.0 collective-permute-done.24.refs_5_
  108.8 1.5 collective-permute-start.26
  110.4 7.7 %collective-permute-done.25.refs_6_ = bf16[144,512]{1,0:T(8,128)(2,1)S(1)} collective-permute-done((bf16[144,512]{1,0:T(8,128)(2,1)S(1)}, bf16[144,512]{1,0:T(8,128)(2,1)S(1)}, u32[]{:S(2)}, u32[]{:S(2)}) %collective-permute-start.25) | collective-permute-done | bytes 147488 | tf_op jit(solution)/shard_map/ppermute | solution.py:323
  118.1 0.0 collective-permute-done.26.refs_7_
  118.1 3.4 %copy-done.1 = bf16[1024,4096]{1,0:T(8,128)(2,1)S(1)} copy-done((bf16[1024,4096]{1,0:T(8,128)(2,1)S(1)}, bf16[1024,4096]{1,0:T(8,128)(2,1)}, u32[]{:S(2)}) %copy-start.1) | copy-done | bytes 8388632
  121.5 3.9 %project.3 = (bf16[128,1024]{1,0:T(8,128)(2,1)S(1)}, bf16[128,1024]{1,0:T(8,128)(2,1)S(1)}, bf16[128,1024]{1,0:T(8,128)(2,1)S(1)}, f32[128,1024]{1,0:T(8,128)S(1)}) custom-call(s32[2]{0:T(128)S(1)} %pad_add_fusion.meta, bf16[144,512]{1,0:T(8,128)(2,1)S(1)} %copy-done.5, bf16[144,512]{1,0:T(8,128)(2,1)S(1)} %collective-permute-done.20.refs_1_, ...), custom_call_target="tpu_custom_call" | custom-call | flops 1073741824 | bytes 8388608 | tf_op jit(solution)/shard_map/project/pallas_call | solution.py:292
  125.4 3.5 %collective-permute-start.27 = (bf16[128,1024]{1,0:T(8,128)(2,1)S(1)}, bf16[128,1024]{1,0:T(8,128)(2,1)S(1)}, u32[]{:S(2)}, u32[]{:S(2)}) collective-permute-start(bf16[128,1024]{1,0:T(8,128)(2,1)S(1)} %get-tuple-element.56), channel_id=1, source_target_pairs={{0,3},{1,2},{2,1},{3,0},{4,7},{5,6},{6,5},{7,4},{8,11},{9,10},{10,... | collective-permute-start | bytes 786440 | tf_op jit(solution)/shard_map/ppermute | solution.py:323
  128.9 0.0 collective-permute-start.28
  128.9 0.0 collective-permute-done.17
  128.9 0.9 collective-permute-start.29
  129.8 12.9 %collective-permute-done.18 = bf16[128,1024]{1,0:T(8,128)(2,1)S(1)} collective-permute-done((bf16[128,1024]{1,0:T(8,128)(2,1)S(1)}, bf16[128,1024]{1,0:T(8,128)(2,1)S(1)}, u32[]{:S(2)}, u32[]{:S(2)}) %collective-permute-start.18) | collective-permute-done | bytes 262176 | tf_op jit(solution)/shard_map/ppermute | solution.py:323
  142.8 0.1 convert_add_fusion.1
  142.9 10.6 %collective-permute-done.28 = bf16[128,1024]{1,0:T(8,128)(2,1)S(1)} collective-permute-done((bf16[128,1024]{1,0:T(8,128)(2,1)S(1)}, bf16[128,1024]{1,0:T(8,128)(2,1)S(1)}, u32[]{:S(2)}, u32[]{:S(2)}) %collective-permute-start.28) | collective-permute-done | bytes 262176 | tf_op jit(solution)/shard_map/ppermute | solution.py:323
  153.5 0.1 convert_add_fusion
  153.7 1.1 pad_maximum_fusion
  (39 shorter events, 0.1 us)
Async XLA Ops:
  0.0 3.7 %copy-start.3 = (bf16[2048,1024]{1,0:T(8,128)(2,1)S(1)}, bf16[2048,1024]{1,0:T(8,128)(2,1)}, u32[]{:S(2)}) copy-start(bf16[2048,1024]{1,0:T(8,128)(2,1)} %own_v.1) | copy-start | bytes 12582916
  0.0 5.3 %copy-start.8 = (bf16[256,1024]{1,0:T(8,128)(2,1)S(1)}, bf16[256,1024]{1,0:T(8,128)(2,1)}, u32[]{:S(2)}) copy-start(bf16[256,1024]{1,0:T(8,128)(2,1)} %param.5) | copy-start | bytes 1572868
  0.0 8.5 %copy-start.10 = (s32[8]{0:T(128)S(1)}, s32[8]{0:T(128)}, u32[]{:S(2)}) copy-start(s32[8]{0:T(128)} %param.8) | copy-start | bytes 100
  3.3 13.2 %collective-permute-start.8 = (bf16[2048,512]{1,0:T(8,128)(2,1)}, bf16[2048,512]{1,0:T(8,128)(2,1)S(1)}, u32[]{:S(2)}, u32[]{:S(2)}) collective-permute-start(bf16[2048,512]{1,0:T(8,128)(2,1)} %constant_dynamic-slice_fusion.1), channel_id=1, source_target_pairs={{0,4},{4,0},{8,12},{12,8},{16,20},{20,16},{24,28},{28,24},{1,5},{5... | collective-permute-start | bytes 6291464 | tf_op jit(solution)/shard_map/ppermute | solution.py:323
  5.3 13.3 %collective-permute-start.9 = (bf16[2048,512]{1,0:T(8,128)(2,1)}, bf16[2048,512]{1,0:T(8,128)(2,1)}, u32[]{:S(2)}, u32[]{:S(2)}) collective-permute-start(bf16[2048,512]{1,0:T(8,128)(2,1)} %constant_dynamic-slice_fusion), channel_id=1, source_target_pairs={{0,4},{4,0},{8,12},{12,8},{16,20},{20,16},{24,28},{28,24},{1,5},{5... | collective-permute-start | bytes 6291464 | tf_op jit(solution)/shard_map/ppermute | solution.py:323
  5.4 27.8 %copy-start.9 = (bf16[256,512]{1,0:T(8,128)(2,1)}, bf16[256,512]{1,0:T(8,128)(2,1)S(1)}, u32[]{:S(2)}) copy-start(bf16[256,512]{1,0:T(8,128)(2,1)S(1)} %get-tuple-element.62.refs_0_) | copy-start | bytes 786436
  5.4 5.5 %collective-permute-start.1 = (bf16[256,512]{1,0:T(8,128)(2,1)S(1)}, bf16[256,512]{1,0:T(8,128)(2,1)S(1)}, u32[]{:S(2)}, u32[]{:S(2)}) collective-permute-start(bf16[256,512]{1,0:T(8,128)(2,1)S(1)} %get-tuple-element.61), channel_id=1, source_target_pairs={{0,4},{4,0},{8,12},{12,8},{16,20},{20,16},{24,28},{28,24},{1,5},{5... | collective-permute-start | bytes 786440 | tf_op jit(solution)/shard_map/ppermute | solution.py:323
  5.9 9.7 %collective-permute-start.2 = (bf16[256,512]{1,0:T(8,128)(2,1)S(1)}, bf16[256,512]{1,0:T(8,128)(2,1)S(1)}, u32[]{:S(2)}, u32[]{:S(2)}) collective-permute-start(bf16[256,512]{1,0:T(8,128)(2,1)S(1)} %get-tuple-element.62.refs_0_), channel_id=1, source_target_pairs={{0,8},{4,12},{8,0},{12,4},{16,24},{20,28},{24,16},{28,20},{1,9},{5... | collective-permute-start | bytes 786440 | tf_op jit(solution)/shard_map/ppermute | solution.py:323
  8.5 2.4 %collective-permute-start = (s32[8]{0:T(128)S(1)}, s32[8]{0:T(128)S(1)}, u32[]{:S(2)}, u32[]{:S(2)}) collective-permute-start(s32[8]{0:T(128)S(1)} %copy-done.10), channel_id=1, source_target_pairs={{0,4},{4,0},{8,12},{12,8},{16,20},{20,16},{24,28},{28,24},{1,5},{5... | collective-permute-start | bytes 104 | tf_op jit(solution)/shard_map/ppermute | solution.py:323
  10.9 23.4 %collective-permute-start.3 = (bf16[256,512]{1,0:T(8,128)(2,1)S(1)}, bf16[256,512]{1,0:T(8,128)(2,1)}, u32[]{:S(2)}, u32[]{:S(2)}) collective-permute-start(bf16[256,512]{1,0:T(8,128)(2,1)S(1)} %get-tuple-element.61), channel_id=1, source_target_pairs={{0,12},{4,8},{8,4},{12,0},{16,28},{20,24},{24,20},{28,16},{1,13},{... | collective-permute-start | bytes 786440 | tf_op jit(solution)/shard_map/ppermute | solution.py:323
  10.9 22.3 %copy-start.11 = (bf16[256,512]{1,0:T(8,128)(2,1)}, bf16[256,512]{1,0:T(8,128)(2,1)S(1)}, u32[]{:S(2)}) copy-start(bf16[256,512]{1,0:T(8,128)(2,1)S(1)} %collective-permute-done.1.refs_1_) | copy-start | bytes 786436
  10.9 23.4 %collective-permute-start.4 = (bf16[256,512]{1,0:T(8,128)(2,1)S(1)}, bf16[256,512]{1,0:T(8,128)(2,1)}, u32[]{:S(2)}, u32[]{:S(2)}) collective-permute-start(bf16[256,512]{1,0:T(8,128)(2,1)S(1)} %get-tuple-element.62.refs_0_), channel_id=1, source_target_pairs={{0,16},{4,20},{8,24},{12,28},{16,0},{20,4},{24,8},{28,12},{1,17},{... | collective-permute-start | bytes 786440 | tf_op jit(solution)/shard_map/ppermute | solution.py:323
  15.7 17.6 %copy-start.12 = (bf16[256,512]{1,0:T(8,128)(2,1)}, bf16[256,512]{1,0:T(8,128)(2,1)S(1)}, u32[]{:S(2)}) copy-start(bf16[256,512]{1,0:T(8,128)(2,1)S(1)} %collective-permute-done.2.refs_2_) | copy-start | bytes 786436
  15.7 21.3 %collective-permute-start.5 = (bf16[256,512]{1,0:T(8,128)(2,1)S(1)}, bf16[256,512]{1,0:T(8,128)(2,1)}, u32[]{:S(2)}, u32[]{:S(2)}) collective-permute-start(bf16[256,512]{1,0:T(8,128)(2,1)S(1)} %get-tuple-element.61), channel_id=1, source_target_pairs={{0,20},{4,16},{8,28},{12,24},{16,4},{20,0},{24,12},{28,8},{1,21},{... | collective-permute-start | bytes 786440 | tf_op jit(solution)/shard_map/ppermute | solution.py:323
  16.5 20.5 %collective-permute-start.6 = (bf16[256,512]{1,0:T(8,128)(2,1)S(1)}, bf16[256,512]{1,0:T(8,128)(2,1)}, u32[]{:S(2)}, u32[]{:S(2)}) collective-permute-start(bf16[256,512]{1,0:T(8,128)(2,1)S(1)} %get-tuple-element.62.refs_0_), channel_id=1, source_target_pairs={{0,24},{4,28},{8,16},{12,20},{16,8},{20,12},{24,0},{28,4},{1,25},{... | collective-permute-start | bytes 786440 | tf_op jit(solution)/shard_map/ppermute | solution.py:323
  18.6 18.3 %collective-permute-start.7 = (bf16[256,512]{1,0:T(8,128)(2,1)S(1)}, bf16[256,512]{1,0:T(8,128)(2,1)}, u32[]{:S(2)}, u32[]{:S(2)}) collective-permute-start(bf16[256,512]{1,0:T(8,128)(2,1)S(1)} %get-tuple-element.61), channel_id=1, source_target_pairs={{0,28},{4,24},{8,20},{12,16},{16,12},{20,8},{24,4},{28,0},{1,29},{... | collective-permute-start | bytes 786440 | tf_op jit(solution)/shard_map/ppermute | solution.py:323
  20.8 2.2 %copy-start.2 = (bf16[2048,1024]{1,0:T(8,128)(2,1)S(1)}, bf16[2048,1024]{1,0:T(8,128)(2,1)}, u32[]{:S(2)}) copy-start(bf16[2048,1024]{1,0:T(8,128)(2,1)} %own_k.1) | copy-start | bytes 12582916
  23.0 2.2 %copy-start.4 = (bf16[2048,1024]{1,0:T(8,128)(2,1)S(1)}, bf16[2048,1024]{1,0:T(8,128)(2,1)}, u32[]{:S(2)}) copy-start(bf16[2048,1024]{1,0:T(8,128)(2,1)} %own_v.1) | copy-start | bytes 12582916
  33.2 1.1 copy-start.7
  58.3 6.8 %collective-permute-start.10 = (bf16[144,512]{1,0:T(8,128)(2,1)}, bf16[144,512]{1,0:T(8,128)(2,1)S(1)}, u32[]{:S(2)}, u32[]{:S(2)}) collective-permute-start(bf16[144,512]{1,0:T(8,128)(2,1)} %get-tuple-element.36), channel_id=1, source_target_pairs={{0,8},{4,12},{8,0},{12,4},{16,24},{20,28},{24,16},{28,20},{1,9},{5... | collective-permute-start | bytes 442376 | tf_op jit(solution)/shard_map/ppermute | solution.py:323
  60.5 9.0 %collective-permute-start.11 = (bf16[144,512]{1,0:T(8,128)(2,1)}, bf16[144,512]{1,0:T(8,128)(2,1)S(1)}, u32[]{:S(2)}, u32[]{:S(2)}) collective-permute-start(bf16[144,512]{1,0:T(8,128)(2,1)} %get-tuple-element.37), channel_id=1, source_target_pairs={{0,16},{4,20},{8,24},{12,28},{16,0},{20,4},{24,8},{28,12},{1,17},{... | collective-permute-start | bytes 442376 | tf_op jit(solution)/shard_map/ppermute | solution.py:323
  61.8 29.0 %collective-permute-start.12 = (bf16[144,512]{1,0:T(8,128)(2,1)}, bf16[144,512]{1,0:T(8,128)(2,1)S(1)}, u32[]{:S(2)}, u32[]{:S(2)}) collective-permute-start(bf16[144,512]{1,0:T(8,128)(2,1)} %get-tuple-element.38), channel_id=1, source_target_pairs={{0,24},{4,28},{8,16},{12,20},{16,8},{20,12},{24,0},{28,4},{1,25},{... | collective-permute-start | bytes 442376 | tf_op jit(solution)/shard_map/ppermute | solution.py:323
  62.0 31.0 %collective-permute-start.13 = (bf16[144,512]{1,0:T(8,128)(2,1)}, bf16[144,512]{1,0:T(8,128)(2,1)S(1)}, u32[]{:S(2)}, u32[]{:S(2)}) collective-permute-start(bf16[144,512]{1,0:T(8,128)(2,1)} %get-tuple-element.39), channel_id=1, source_target_pairs={{0,4},{4,0},{8,12},{12,8},{16,20},{20,16},{24,28},{28,24},{1,5},{5... | collective-permute-start | bytes 442376 | tf_op jit(solution)/shard_map/ppermute | solution.py:323
  62.0 31.0 %collective-permute-start.14 = (bf16[144,512]{1,0:T(8,128)(2,1)}, bf16[144,512]{1,0:T(8,128)(2,1)S(1)}, u32[]{:S(2)}, u32[]{:S(2)}) collective-permute-start(bf16[144,512]{1,0:T(8,128)(2,1)} %get-tuple-element.40), channel_id=1, source_target_pairs={{0,12},{4,8},{8,4},{12,0},{16,28},{20,24},{24,20},{28,16},{1,13},{... | collective-permute-start | bytes 442376 | tf_op jit(solution)/shard_map/ppermute | solution.py:323
  65.2 29.4 %collective-permute-start.15 = (bf16[144,512]{1,0:T(8,128)(2,1)}, bf16[144,512]{1,0:T(8,128)(2,1)S(1)}, u32[]{:S(2)}, u32[]{:S(2)}) collective-permute-start(bf16[144,512]{1,0:T(8,128)(2,1)} %get-tuple-element.41), channel_id=1, source_target_pairs={{0,20},{4,16},{8,28},{12,24},{16,4},{20,0},{24,12},{28,8},{1,21},{... | collective-permute-start | bytes 442376 | tf_op jit(solution)/shard_map/ppermute | solution.py:323
  69.5 27.7 %copy-start.6 = (bf16[144,512]{1,0:T(8,128)(2,1)S(1)}, bf16[144,512]{1,0:T(8,128)(2,1)}, u32[]{:S(2)}) copy-start(bf16[144,512]{1,0:T(8,128)(2,1)} %get-tuple-element.35.refs_0_) | copy-start | bytes 442372
  69.5 26.4 %collective-permute-start.16 = (bf16[144,512]{1,0:T(8,128)(2,1)}, bf16[144,512]{1,0:T(8,128)(2,1)S(1)}, u32[]{:S(2)}, u32[]{:S(2)}) collective-permute-start(bf16[144,512]{1,0:T(8,128)(2,1)} %get-tuple-element.42), channel_id=1, source_target_pairs={{0,28},{4,24},{8,20},{12,16},{16,12},{20,8},{24,4},{28,0},{1,29},{... | collective-permute-start | bytes 442376 | tf_op jit(solution)/shard_map/ppermute | solution.py:323
  90.9 13.4 %collective-permute-start.20 = (bf16[144,512]{1,0:T(8,128)(2,1)}, bf16[144,512]{1,0:T(8,128)(2,1)S(1)}, u32[]{:S(2)}, u32[]{:S(2)}) collective-permute-start(bf16[144,512]{1,0:T(8,128)(2,1)} %get-tuple-element.48), channel_id=1, source_target_pairs={{0,8},{4,12},{8,0},{12,4},{16,24},{20,28},{24,16},{28,20},{1,9},{5... | collective-permute-start | bytes 442376 | tf_op jit(solution)/shard_map/ppermute | solution.py:323
  93.0 15.1 %collective-permute-start.21 = (bf16[144,512]{1,0:T(8,128)(2,1)}, bf16[144,512]{1,0:T(8,128)(2,1)S(1)}, u32[]{:S(2)}, u32[]{:S(2)}) collective-permute-start(bf16[144,512]{1,0:T(8,128)(2,1)} %get-tuple-element.49), channel_id=1, source_target_pairs={{0,16},{4,20},{8,24},{12,28},{16,0},{20,4},{24,8},{28,12},{1,17},{... | collective-permute-start | bytes 442376 | tf_op jit(solution)/shard_map/ppermute | solution.py:323
  93.0 15.1 %collective-permute-start.22 = (bf16[144,512]{1,0:T(8,128)(2,1)}, bf16[144,512]{1,0:T(8,128)(2,1)S(1)}, u32[]{:S(2)}, u32[]{:S(2)}) collective-permute-start(bf16[144,512]{1,0:T(8,128)(2,1)} %get-tuple-element.50), channel_id=1, source_target_pairs={{0,24},{4,28},{8,16},{12,20},{16,8},{20,12},{24,0},{28,4},{1,25},{... | collective-permute-start | bytes 442376 | tf_op jit(solution)/shard_map/ppermute | solution.py:323
  94.6 14.3 %collective-permute-start.23 = (bf16[144,512]{1,0:T(8,128)(2,1)}, bf16[144,512]{1,0:T(8,128)(2,1)S(1)}, u32[]{:S(2)}, u32[]{:S(2)}) collective-permute-start(bf16[144,512]{1,0:T(8,128)(2,1)} %get-tuple-element.51), channel_id=1, source_target_pairs={{0,4},{4,0},{8,12},{12,8},{16,20},{20,16},{24,28},{28,24},{1,5},{5... | collective-permute-start | bytes 442376 | tf_op jit(solution)/shard_map/ppermute | solution.py:323
  95.9 12.9 %collective-permute-start.24 = (bf16[144,512]{1,0:T(8,128)(2,1)}, bf16[144,512]{1,0:T(8,128)(2,1)S(1)}, u32[]{:S(2)}, u32[]{:S(2)}) collective-permute-start(bf16[144,512]{1,0:T(8,128)(2,1)} %get-tuple-element.52), channel_id=1, source_target_pairs={{0,12},{4,8},{8,4},{12,0},{16,28},{20,24},{24,20},{28,16},{1,13},{... | collective-permute-start | bytes 442376 | tf_op jit(solution)/shard_map/ppermute | solution.py:323
  97.3 3.4 %copy-start = (bf16[1024,4096]{1,0:T(8,128)(2,1)S(1)}, bf16[1024,4096]{1,0:T(8,128)(2,1)}, u32[]{:S(2)}) copy-start(bf16[1024,4096]{1,0:T(8,128)(2,1)} %refs_8_.3) | copy-start | bytes 25165828
  100.6 8.2 %copy-start.14 = (bf16[144,512]{1,0:T(8,128)(2,1)S(1)}, bf16[144,512]{1,0:T(8,128)(2,1)}, u32[]{:S(2)}) copy-start(bf16[144,512]{1,0:T(8,128)(2,1)} %get-tuple-element.53) | copy-start | bytes 442372
  100.6 8.2 %copy-start.13 = (bf16[144,512]{1,0:T(8,128)(2,1)S(1)}, bf16[144,512]{1,0:T(8,128)(2,1)}, u32[]{:S(2)}) copy-start(bf16[144,512]{1,0:T(8,128)(2,1)} %get-tuple-element.54) | copy-start | bytes 442372
  100.6 17.5 %copy-start.5 = (bf16[144,512]{1,0:T(8,128)(2,1)S(1)}, bf16[144,512]{1,0:T(8,128)(2,1)}, u32[]{:S(2)}) copy-start(bf16[144,512]{1,0:T(8,128)(2,1)} %get-tuple-element.47.refs_0_) | copy-start | bytes 442372
  104.3 24.6 %collective-permute-start.17 = (bf16[128,1024]{1,0:T(8,128)(2,1)S(1)}, bf16[128,1024]{1,0:T(8,128)(2,1)S(1)}, u32[]{:S(2)}, u32[]{:S(2)}) collective-permute-start(bf16[128,1024]{1,0:T(8,128)(2,1)S(1)} %get-tuple-element.44), channel_id=1, source_target_pairs={{0,3},{1,2},{2,1},{3,0},{4,7},{5,6},{6,5},{7,4},{8,11},{9,10},{10,... | collective-permute-start | bytes 786440 | tf_op jit(solution)/shard_map/ppermute | solution.py:323
  108.1 34.7 %collective-permute-start.18 = (bf16[128,1024]{1,0:T(8,128)(2,1)S(1)}, bf16[128,1024]{1,0:T(8,128)(2,1)S(1)}, u32[]{:S(2)}, u32[]{:S(2)}) collective-permute-start(bf16[128,1024]{1,0:T(8,128)(2,1)S(1)} %get-tuple-element.45), channel_id=1, source_target_pairs={{0,2},{1,3},{2,0},{3,1},{4,6},{5,7},{6,4},{7,5},{8,10},{9,11},{10,... | collective-permute-start | bytes 786440 | tf_op jit(solution)/shard_map/ppermute | solution.py:323
  108.1 34.7 %collective-permute-start.19 = (bf16[128,1024]{1,0:T(8,128)(2,1)S(1)}, bf16[128,1024]{1,0:T(8,128)(2,1)S(1)}, u32[]{:S(2)}, u32[]{:S(2)}) collective-permute-start(bf16[128,1024]{1,0:T(8,128)(2,1)S(1)} %get-tuple-element.46), channel_id=1, source_target_pairs={{0,1},{1,0},{2,3},{3,2},{4,5},{5,4},{6,7},{7,6},{8,9},{9,8},{10,11... | collective-permute-start | bytes 786440 | tf_op jit(solution)/shard_map/ppermute | solution.py:323
  108.8 9.3 %collective-permute-start.25 = (bf16[144,512]{1,0:T(8,128)(2,1)S(1)}, bf16[144,512]{1,0:T(8,128)(2,1)S(1)}, u32[]{:S(2)}, u32[]{:S(2)}) collective-permute-start(bf16[144,512]{1,0:T(8,128)(2,1)S(1)} %copy-done.14), channel_id=1, source_target_pairs={{0,20},{4,16},{8,28},{12,24},{16,4},{20,0},{24,12},{28,8},{1,21},{... | collective-permute-start | bytes 442376 | tf_op jit(solution)/shard_map/ppermute | solution.py:323
  108.8 9.3 %collective-permute-start.26 = (bf16[144,512]{1,0:T(8,128)(2,1)S(1)}, bf16[144,512]{1,0:T(8,128)(2,1)S(1)}, u32[]{:S(2)}, u32[]{:S(2)}) collective-permute-start(bf16[144,512]{1,0:T(8,128)(2,1)S(1)} %copy-done.13), channel_id=1, source_target_pairs={{0,28},{4,24},{8,20},{12,16},{16,12},{20,8},{24,4},{28,0},{1,29},{... | collective-permute-start | bytes 442376 | tf_op jit(solution)/shard_map/ppermute | solution.py:323
  118.1 3.4 %copy-start.1 = (bf16[1024,4096]{1,0:T(8,128)(2,1)S(1)}, bf16[1024,4096]{1,0:T(8,128)(2,1)}, u32[]{:S(2)}) copy-start(bf16[1024,4096]{1,0:T(8,128)(2,1)} %refs_8_.3) | copy-start | bytes 25165828
  125.4 17.5 %collective-permute-start.27 = (bf16[128,1024]{1,0:T(8,128)(2,1)S(1)}, bf16[128,1024]{1,0:T(8,128)(2,1)S(1)}, u32[]{:S(2)}, u32[]{:S(2)}) collective-permute-start(bf16[128,1024]{1,0:T(8,128)(2,1)S(1)} %get-tuple-element.56), channel_id=1, source_target_pairs={{0,3},{1,2},{2,1},{3,0},{4,7},{5,6},{6,5},{7,4},{8,11},{9,10},{10,... | collective-permute-start | bytes 786440 | tf_op jit(solution)/shard_map/ppermute | solution.py:323
  128.9 24.7 %collective-permute-start.28 = (bf16[128,1024]{1,0:T(8,128)(2,1)S(1)}, bf16[128,1024]{1,0:T(8,128)(2,1)S(1)}, u32[]{:S(2)}, u32[]{:S(2)}) collective-permute-start(bf16[128,1024]{1,0:T(8,128)(2,1)S(1)} %get-tuple-element.57), channel_id=1, source_target_pairs={{0,2},{1,3},{2,0},{3,1},{4,6},{5,7},{6,4},{7,5},{8,10},{9,11},{10,... | collective-permute-start | bytes 786440 | tf_op jit(solution)/shard_map/ppermute | solution.py:323
  128.9 24.6 %collective-permute-start.29 = (bf16[128,1024]{1,0:T(8,128)(2,1)S(1)}, bf16[128,1024]{1,0:T(8,128)(2,1)S(1)}, u32[]{:S(2)}, u32[]{:S(2)}) collective-permute-start(bf16[128,1024]{1,0:T(8,128)(2,1)S(1)} %get-tuple-element.58), channel_id=1, source_target_pairs={{0,1},{1,0},{2,3},{3,2},{4,5},{5,4},{6,7},{7,6},{8,9},{9,8},{10,11... | collective-permute-start | bytes 786440 | tf_op jit(solution)/shard_map/ppermute | solution.py:323

commit v2 on v1

v2 whole, which is shorter than its diff:
```python
import functools
import math

import jax
import jax.numpy as jnp
from jax import lax
from jax.experimental import pallas as pl
from jax.experimental.pallas import tpu as pltpu
from jax.sharding import PartitionSpec as P

HD = 128
SPAN = 256
STEP = 16
UNIT = 256
BLOCK = 4 * UNIT
SUB = 256
SCALE = math.log2(math.e) / math.sqrt(HD)
NT = (((1,), (1,)), ((), ()))
NN = (((1,), (0,)), ((), ()))
MIB = 2**20
VMEM = 58 * MIB


def groups_of(rows):
    half = rows // 2
    size = min(half, HD)
    return [
        (core * half + at, min(size, half - at)) for core in range(2) for at in range(0, half, size)
    ]


def stat_rows(rows):
    return (3 * len(groups_of(rows)) + 15) // 16 * 16


def eye_of(size):
    return lax.broadcasted_iota(jnp.int32, (size, HD), 0) == (
        lax.broadcasted_iota(jnp.int32, (size, HD), 1)
    )


def round_up(size):
    return (size + STEP - 1) // STEP * STEP


def pack(spans, own, got, out, fill):
    here = own.shape[0] // SPAN
    rows = lax.broadcasted_iota(jnp.int32, (STEP, HD), 0)
    at = jnp.int32(0)
    for passage in range(2 * here):
        source = own if passage < here else got
        base = passage % here * SPAN
        size = spans[passage]
        out[pl.ds(pl.multiple_of(at, STEP), SPAN), :] = source[base : base + SPAN, :]
        edge = jnp.minimum(size // STEP * STEP, SPAN - STEP)
        last = source[pl.ds(pl.multiple_of(base + edge, STEP), STEP), :].astype(jnp.float32)
        if fill:
            filler = jnp.broadcast_to(
                source[base : base + STEP, :].astype(jnp.float32)[:1, :], (STEP, HD)
            )
        else:
            filler = jnp.zeros((STEP, HD), jnp.float32)
        out[pl.ds(pl.multiple_of(at + edge, STEP), STEP), :] = jnp.where(
            rows + edge < size, last, filler
        ).astype(jnp.bfloat16)
        at = at + round_up(size)
    filler = filler.astype(jnp.bfloat16)
    for i in range(UNIT // STEP):
        out[pl.ds(pl.multiple_of(at + i * STEP, STEP), STEP), :] = filler


def mark(spans, passages, out):
    rows = lax.broadcasted_iota(jnp.int32, (STEP, HD), 0)
    at = jnp.int32(0)
    for passage in range(passages):
        size = spans[passage]
        out[pl.ds(pl.multiple_of(at, STEP), SPAN), :] = jnp.ones((SPAN, HD), jnp.bfloat16)
        edge = jnp.minimum(size // STEP * STEP, SPAN - STEP)
        out[pl.ds(pl.multiple_of(at + edge, STEP), STEP), :] = jnp.where(
            rows + edge < size, 1.0, 0.0
        ).astype(jnp.bfloat16)
        at = at + round_up(size)
    out[pl.ds(pl.multiple_of(at, STEP), UNIT), :] = jnp.zeros((UNIT, HD), jnp.bfloat16)


def attend_kernel(blocks, tiles, first, afters, spans, meta, *refs):
    refs = list(refs)
    take = lambda n: [refs.pop(0) for _ in range(n)]
    q_refs = take(blocks)
    if first:
        own_k, got_k, own_v, got_v = take(4)
    else:
        k_ref, v_ref = take(2)
    take(afters)
    o_refs = take(blocks)
    if first:
        k_ref, v_ref = take(2)
    q_all, m_ref, s_even, s_odd, top_even, top_odd, acc = refs
    rows = q_refs[0].shape[0]
    step = pl.program_id(0)
    passages = (k_ref.shape[0] - UNIT) // SPAN
    count = sum(round_up(spans[i]) for i in range(passages))
    units = (count + UNIT - 1) // UNIT
    turns = units // (BLOCK // UNIT)
    rest = units - turns * (BLOCK // UNIT)
    total = blocks * rows
    sub = min(SUB, total)

    def score(at, scores, top, part):
        s = lax.dot_general(
            q_all[part, :], k_ref[at, :], NT, preferred_element_type=jnp.float32
        )
        scores[part, at] = s
        most = top[part, :]
        for i in range(s.shape[1] // HD):
            most = jnp.maximum(most, s[:, i * HD : (i + 1) * HD])
        top[part, :] = most

    def weigh(at, scores, top, part):
        value = jnp.concatenate([v_ref[at, :], m_ref[at, :]], axis=1)
        most = top[part, :]
        s = scores[part, at]
        weights = jnp.concatenate(
            [
                jnp.exp2((s[:, i * HD : (i + 1) * HD] - most) * SCALE).astype(jnp.bfloat16)
                for i in range(s.shape[1] // HD)
            ],
            axis=1,
        )
        acc[part, :] += lax.dot_general(
            weights, value, NN, preferred_element_type=jnp.float32
        )

    def run(now, then):
        if then is not None:
            scores_then, top_then = then
            if first:
                pack(spans, own_v, got_v, v_ref, False)
            top_then[...] = jnp.broadcast_to(
                jnp.max(top_then[...], axis=1, keepdims=True), top_then.shape
            )
            acc[...] = jnp.zeros_like(acc)
        if now is not None:
            scores_now, top_now = now
            if first:
                pack(spans, own_k, got_k, k_ref, True)
            top_now[...] = jnp.full(top_now.shape, -3e38, jnp.float32)
            for b in range(blocks):
                q_all[b * rows : (b + 1) * rows, :] = q_refs[b][...]

        def body(start, size):
            at = pl.ds(pl.multiple_of(start, UNIT), size)
            for r in range(total // sub):
                part = pl.ds(r * sub, sub)
                if now is not None:
                    score(at, scores_now, top_now, part)
                if then is not None:
                    weigh(at, scores_then, top_then, part)

        @pl.loop(0, turns)
        def _(turn):
            body(turn * BLOCK, BLOCK)

        @pl.loop(0, rest)
        def _(turn):
            body(turns * BLOCK + turn * UNIT, UNIT)

        if then is not None:
            for b in range(blocks):
                finish(b, top_then)

    def finish(b, top):
        index = lax.broadcasted_iota(jnp.int32, (stat_rows(rows), HD), 0)
        packed = jnp.zeros(index.shape, jnp.float32)
        for u, (start, size) in enumerate(groups_of(rows)):
            part = pl.ds(b * rows + start, size)
            sums = acc[part, HD:]
            o_refs[b][start : start + size, :] = (acc[part, :HD] / sums).astype(jnp.bfloat16)
            logs = top[part, :] * SCALE + jnp.log2(sums)
            line = jnp.sum(jnp.where(eye_of(size), logs, 0.0), axis=0, keepdims=True)
            high = line.astype(jnp.bfloat16).astype(jnp.float32)
            middle = (line - high).astype(jnp.bfloat16).astype(jnp.float32)
            for i, term in enumerate((high, middle, line - high - middle)):
                packed = jnp.where(index == 3 * u + i, term, packed)
        o_refs[b][rows:, :] = packed.astype(jnp.bfloat16)

    even, odd = (s_even, top_even), (s_odd, top_odd)
    is_even = lax.rem(step, 2) == 0
    inside = jnp.logical_and(step > 0, step < tiles)

    @pl.when(step == 0)
    def _():
        mark(spans, passages, m_ref)
        run(even, None)

    if tiles > 1:

        @pl.when(jnp.logical_and(inside, is_even))
        def _():
            run(even, odd)

        @pl.when(jnp.logical_and(inside, jnp.logical_not(is_even)))
        def _():
            run(odd, even)

    @pl.when(step == tiles)
    def _():
        run(None, odd if tiles % 2 == 0 else even)


def attend(spans, meta, queries, raw, packed, after=()):
    first = packed is None
    blocks = len(queries)
    rows, width = queries[0].shape
    heads = width // HD
    tokens = raw[1].shape[0] if first else (packed[0].shape[0] - UNIT) // 2
    size = 2 * tokens + UNIT
    tall = rows + stat_rows(rows)
    now = lambda t: jnp.minimum(t, heads - 1)
    then = lambda t: jnp.maximum(t - 1, 0)
    total = blocks * rows
    packed_specs = [
        pl.BlockSpec((size, HD), lambda t, n, m: (0, now(t))),
        pl.BlockSpec((size, HD), lambda t, n, m: (0, then(t))),
    ]
    raw_specs = [
        pl.BlockSpec((tokens, HD), lambda t, n, m: (0, m[0] * heads + now(t))),
        pl.BlockSpec((tokens, HD), lambda t, n, m: (0, now(t))),
        pl.BlockSpec((tokens, HD), lambda t, n, m: (0, m[0] * heads + then(t))),
        pl.BlockSpec((tokens, HD), lambda t, n, m: (0, then(t))),
    ]
    results = pl.pallas_call(
        functools.partial(attend_kernel, blocks, heads, first, len(after)),
        grid_spec=pltpu.PrefetchScalarGridSpec(
            num_scalar_prefetch=2,
            grid=(heads + 1,),
            in_specs=[pl.BlockSpec((rows, HD), lambda t, n, m: (0, now(t)))] * blocks
            + (raw_specs if first else packed_specs)
            + [pl.BlockSpec(memory_space=pl.ANY)] * len(after),
            out_specs=[pl.BlockSpec((tall, HD), lambda t, n, m: (0, then(t)))] * blocks
            + (packed_specs if first else []),
            scratch_shapes=[
                pltpu.VMEM((total, HD), jnp.bfloat16),
                pltpu.VMEM((size, HD), jnp.bfloat16),
                pltpu.VMEM((total, size), jnp.float32),
                pltpu.VMEM((total, size), jnp.float32),
                pltpu.VMEM((total, HD), jnp.float32),
                pltpu.VMEM((total, HD), jnp.float32),
                pltpu.VMEM((total, 2 * HD), jnp.float32),
            ],
        ),
        out_shape=[jax.ShapeDtypeStruct((tall, width), jnp.bfloat16)] * blocks
        + [jax.ShapeDtypeStruct((size, width), jnp.bfloat16)] * (2 if first else 0),
        compiler_params=pltpu.CompilerParams(vmem_limit_bytes=VMEM),
        cost_estimate=pl.CostEstimate(
            flops=4 * total * size * width, bytes_accessed=4 * size * width, transcendentals=0
        ),
        name="attend",
    )(spans, meta, *queries, *(raw if first else packed), *after)
    results = list(results)
    return results[:blocks], tuple(results[blocks:]) if first else packed


def merge_kernel(count, *refs):
    parts, (keep, give) = refs[:count], refs[-2:]
    half, width = keep.shape
    rows = 2 * half
    for u, (start, size) in enumerate(groups_of(rows)):
        eye = eye_of(size)
        out, there = (keep, start) if start < half else (give, start - half)
        for head in range(width // HD):
            cols = slice(head * HD, (head + 1) * HD)
            logs = []
            for part in parts:
                stats = part[rows:, cols].astype(jnp.float32)[3 * u : 3 * u + 3]
                logs.append(stats[0:1] + (stats[1:2] + stats[2:3]))
            most = functools.reduce(jnp.maximum, logs)
            shares = [jnp.exp2(x - most) for x in logs]
            whole = functools.reduce(jnp.add, shares)
            merged = None
            for part, share in zip(parts, shares):
                line = jnp.broadcast_to(share / whole, (size, HD))
                column = jnp.sum(jnp.where(eye, line, 0.0), axis=1, keepdims=True)
                term = part[start : start + size, cols].astype(jnp.float32) * column
                merged = term if merged is None else merged + term
            out[there : there + size, cols] = merged.astype(jnp.bfloat16)


def merge(parts, half, after=()):
    width = parts[0].shape[1]
    shape = jax.ShapeDtypeStruct((half, width), jnp.bfloat16)
    return pl.pallas_call(
        functools.partial(merge_kernel, len(parts)),
        in_specs=[pl.BlockSpec(memory_space=pltpu.VMEM)] * len(parts)
        + [pl.BlockSpec(memory_space=pl.ANY)] * len(after),
        out_specs=[pl.BlockSpec(memory_space=pltpu.VMEM)] * 2,
        out_shape=[shape, shape],
        compiler_params=pltpu.CompilerParams(vmem_limit_bytes=VMEM),
        cost_estimate=pl.CostEstimate(
            flops=0, bytes_accessed=4 * half * width * len(parts), transcendentals=0
        ),
        name="merge",
    )(*parts, *after)


def project_kernel(pieces, meta, keep, got, *refs):
    weights, outs, attended = refs[:pieces], refs[pieces:-1], refs[-1]
    step = pl.program_id(0)
    width = keep.shape[1]

    @pl.when(step == 0)
    def _():
        attended[:, pl.ds(pl.multiple_of(meta[0] * width, HD), width)] = keep[...]
        attended[:, pl.ds(pl.multiple_of((1 - meta[0]) * width, HD), width)] = got[...]

    for i in range(len(outs)):

        @pl.when(step == i)
        def _(i=i):
            deep = weights[0].shape[0]
            outs[i][...] = sum(
                lax.dot_general(
                    attended[:, p * deep : (p + 1) * deep],
                    weight[...],
                    NN,
                    preferred_element_type=jnp.float32,
                )
                for p, weight in enumerate(weights)
            ).astype(outs[i].dtype)


def project(meta, keep, got, out_weight, groups):
    depth, total = out_weight.shape
    rows, width = keep.shape
    cols = total // groups
    whole = pl.BlockSpec((rows, width), lambda t, m: (0, 0))
    pieces = depth // UNIT
    return pl.pallas_call(
        functools.partial(project_kernel, pieces),
        grid_spec=pltpu.PrefetchScalarGridSpec(
            num_scalar_prefetch=1,
            grid=(groups,),
            in_specs=[whole, whole]
            + [
                pl.BlockSpec((UNIT, cols), lambda t, m, p=p: (p, m[1] ^ (groups - 1 - t)))
                for p in range(pieces)
            ],
            out_specs=[pl.BlockSpec((rows, cols), lambda t, m: (0, 0))] * groups,
            scratch_shapes=[pltpu.VMEM((rows, depth), jnp.bfloat16)],
        ),
        out_shape=[
            jax.ShapeDtypeStruct((rows, cols), jnp.bfloat16 if t < groups - 1 else jnp.float32)
            for t in range(groups)
        ],
        compiler_params=pltpu.CompilerParams(vmem_limit_bytes=VMEM),
        cost_estimate=pl.CostEstimate(
            flops=2 * rows * depth * total, bytes_accessed=2 * depth * total, transcendentals=0
        ),
        name="project",
    )(meta, keep, got, *[out_weight] * pieces)


def on_device(queries, keys, values, lengths, out_weight):
    sources = lax.axis_size("ctx")
    groups = lax.axis_size("head")
    core = lax.rem(lax.axis_index("ctx"), 2)
    width = keys.shape[1] // 2
    meta = jnp.stack([core, lax.axis_index("head")]).astype(jnp.int32)

    def swap(x, k, axis="ctx"):
        n = sources if axis == "ctx" else groups
        return lax.ppermute(x, axis, [(i, i ^ k) for i in range(n)])

    def half(x, which):
        return lax.dynamic_slice(x, (0, which * width), (x.shape[0], width))

    def back_to_owners(blocks):
        return [swap(block, 2 * i + 2) for i, block in enumerate(blocks)]

    def finish(parts, after=()):
        keep, give = merge(parts, rows, after)
        return project(meta, keep, swap(give, 1), out_weight, groups)

    def gather(blocks):
        total = blocks[-1]
        for d in range(groups - 1, 0, -1):
            total = total + swap(blocks[groups - 1 - d], d, "head").astype(jnp.float32)
        return total

    rows = queries.shape[0] // 2
    mine = half(queries, core)
    theirs = swap(half(queries, 1 - core), 1)
    ours = [jnp.concatenate([mine[:rows], theirs[:rows]]), jnp.concatenate([mine[rows:], theirs[rows:]])]
    asked = [swap(ours[0], k) for k in range(2, sources, 2)]
    keys_then, values_then, _ = lax.optimization_barrier((keys, values, ours[0]))
    got_k = swap(half(keys_then, 1 - core), 1)
    got_v = swap(half(values_then, 1 - core), 1)
    spans = jnp.concatenate([lengths, swap(lengths, 1)])
    ours[1], _ = lax.optimization_barrier((ours[1], got_v))
    asked_then = [swap(ours[1], k) for k in range(2, sources, 2)]

    raw = (keys, got_k, values, got_v)
    partial, packed = attend(spans, meta, [ours[0]] + asked, raw, None)
    back = [partial[0]] + back_to_owners(partial[1:])
    partial_then, _ = attend(spans, meta, asked_then, raw, packed)
    back_then = back_to_owners(partial_then)
    blocks = finish(back, after=partial_then[:1])
    partial_own, _ = attend(spans, meta, ours[1:], raw, packed, after=blocks[:1])
    blocks_then = finish(partial_own + back_then)
    return jnp.concatenate([gather(blocks), gather(blocks_then)], axis=0)


def solution(mesh):
    in_specs = (P("ctx", "head"), P("ctx", "head"), P("ctx", "head"), P("ctx"), P("head", None))
    out_specs = P("ctx", "head")
    return jax.shard_map(
        on_device, mesh=mesh, in_specs=in_specs, out_specs=out_specs, check_vma=False
    )
```

time: 154 us -> 143 us (0.929)
  waiting for transfers between devices: 42.6 us -> 25.7 us
  Pallas kernels: 58.2 us -> 74.3 us
  starting transfers between devices: 34.4 us -> 27.8 us
  local copies, waits for them, and re-layouts: 17.1 us -> 10.7 us
    ppermute x30 -> x24, waiting for transfers between devices: 42.6 us -> 25.7 us  [swap(): return lax.ppermute(x, axis, [(i, i ^ k) for i in range(n)])]
    pallas_call x5 -> x7, Pallas kernels: 58.2 us -> 74.3 us  [the longest x3 55.6 us: attend(): pl.pallas_call(functools.partial(attend_kernel, blocks, heads, first, len...]
    unnamed x30 -> x38, local copies, waits for them, and re-layouts: 12.2 us -> 5.03 us
    ppermute x30 -> x24, starting transfers between devices: 34.4 us -> 27.8 us  [swap(): return lax.ppermute(x, axis, [(i, i ^ k) for i in range(n)])]
  transfers between devices with their start and end apart: 30 -> 24, of which waited for: 8 -> 5; matrix products, arithmetic and copies ran while one was open for 2% -> 2% of each run, Pallas kernels for 24% -> 52%
where the time goes in v2:
time: 143 us; the launch traced here: 142 us
  Pallas kernels  74.3 us (52%)
  starting transfers between devices  27.8 us (19%)
  waiting for transfers between devices  25.7 us (18%)
  local copies, waits for them, and re-layouts  10.7 us (7%)
  other arithmetic  3.69 us (3%)
    pallas_call x3, Pallas kernels, attend(): pl.pallas_call(functools.partial(attend_kernel, blocks, heads, first, len...  55.6 us
    ppermute x24, starting transfers between devices, swap(): return lax.ppermute(x, axis, [(i, i ^ k) for i in range(n)])  27.8 us
    ppermute x24, waiting for transfers between devices, swap(): return lax.ppermute(x, axis, [(i, i ^ k) for i in range(n)])  25.7 us
    pallas_call x2, Pallas kernels, project(): pl.pallas_call(functools.partial(project_kernel, pieces), grid_spec=pltpu...  13.6 us
    pallas_call x2, Pallas kernels, merge(): pl.pallas_call(functools.partial(merge_kernel, len(parts)), in_specs=[pl....  5.05 us
    unnamed x38, local copies, waits for them, and re-layouts  5.03 us
    dynamic_slice x3, local copies, waits for them, and re-layouts, half(): return lax.dynamic_slice(x, (0, which * width), (x.shape[0], width))  4.54 us
  transfers between devices with their start and end apart: 24, of which 5 were waited for; matrix products, arithmetic and copies ran while one was open for 2% of the time, Pallas kernels for 52%

profile of v2, /device:TPU:0, one launch (start us, length us, event | category | flops | bytes accessed | tf_op | source)
XLA Modules:
  0.0 142.3 jit_solution(14505661168304876720)
XLA Ops:
  0.0 1.0 constant_dynamic-slice_fusion.3
  1.0 0.5 collective-permute-start.1
  1.5 1.1 constant_dynamic-slice_fusion
  2.6 0.0 collective-permute-done.1
  2.7 0.0 copy-start.18
  2.7 3.3 %constant_dynamic-slice_fusion.1 = bf16[2048,512]{1,0:T(8,128)(2,1)} fusion(bf16[2048,1024]{1,0:T(8,128)(2,1)} %refs_6_.1, s32[]{:T(128)S(6)} %select_n.9), kind=kLoop, calls=%fused_computation.6 | loop fusion | bytes 4194308 | tf_op jit(solution)/shard_map/dynamic_slice | solution.py:375
  6.1 0.2 collective-permute-start.6
  6.3 0.2 constant_dynamic-slice_fusion.2
  6.5 0.4 collective-permute-start.5
  6.9 0.2 collective-permute-start
  7.1 2.8 %collective-permute-start.2 = (bf16[256,512]{1,0:T(8,128)(2,1)S(1)}, bf16[256,512]{1,0:T(8,128)(2,1)S(1)}, u32[]{:S(2)}, u32[]{:S(2)}) collective-permute-start(bf16[256,512]{1,0:T(8,128)(2,1)S(1)} %pad_maximum_fusion.1.refs_0_), channel_id=1, source_target_pairs={{0,8},{4,12},{8,0},{12,4},{16,24},{20,28},{24,16},{28,20},{1,9},{5... | collective-permute-start | bytes 786440 | tf_op jit(solution)/shard_map/ppermute | solution.py:372
  9.9 1.5 %collective-permute-start.3 = (bf16[256,512]{1,0:T(8,128)(2,1)S(1)}, bf16[256,512]{1,0:T(8,128)(2,1)S(1)}, u32[]{:S(2)}, u32[]{:S(2)}) collective-permute-start(bf16[256,512]{1,0:T(8,128)(2,1)S(1)} %pad_maximum_fusion.1.refs_0_), channel_id=1, source_target_pairs={{0,16},{4,20},{8,24},{12,28},{16,0},{20,4},{24,8},{28,12},{1,17},{... | collective-permute-start | bytes 786440 | tf_op jit(solution)/shard_map/ppermute | solution.py:372
  11.4 0.0 collective-permute-done
  11.4 2.4 %collective-permute-start.4 = (bf16[256,512]{1,0:T(8,128)(2,1)S(1)}, bf16[256,512]{1,0:T(8,128)(2,1)S(1)}, u32[]{:S(2)}, u32[]{:S(2)}) collective-permute-start(bf16[256,512]{1,0:T(8,128)(2,1)S(1)} %pad_maximum_fusion.1.refs_0_), channel_id=1, source_target_pairs={{0,24},{4,28},{8,16},{12,20},{16,8},{20,12},{24,0},{28,4},{1,25},{... | collective-permute-start | bytes 786440 | tf_op jit(solution)/shard_map/ppermute | solution.py:372
  13.8 0.7 pad_add_fusion.meta
  14.5 0.6 pad_add_fusion.1.spans
  15.2 0.6 collective-permute-start.10
  15.8 1.2 collective-permute-done.2.refs_1_
  17.0 2.1 %collective-permute-start.11 = (bf16[256,512]{1,0:T(8,128)(2,1)S(1)}, bf16[256,512]{1,0:T(8,128)(2,1)S(1)}, u32[]{:S(2)}, u32[]{:S(2)}) collective-permute-start(bf16[256,512]{1,0:T(8,128)(2,1)S(1)} %pad_maximum_fusion.2.refs_0_), channel_id=1, source_target_pairs={{0,16},{4,20},{8,24},{12,28},{16,0},{20,4},{24,8},{28,12},{1,17},{... | collective-permute-start | bytes 786440 | tf_op jit(solution)/shard_map/ppermute | solution.py:372
  19.0 4.7 %collective-permute-done.3.refs_2_ = bf16[256,512]{1,0:T(8,128)(2,1)S(1)} collective-permute-done((bf16[256,512]{1,0:T(8,128)(2,1)S(1)}, bf16[256,512]{1,0:T(8,128)(2,1)S(1)}, u32[]{:S(2)}, u32[]{:S(2)}) %collective-permute-start.3) | collective-permute-done | bytes 262176 | tf_op jit(solution)/shard_map/ppermute | solution.py:372
  23.7 1.2 collective-permute-start.12
  25.0 0.0 collective-permute-done.4.refs_3_
  25.0 0.0 collective-permute-done.5.refs_5_
  25.0 0.7 copy-done.16
  25.7 24.8 %attend.3 = (bf16[272,512]{1,0:T(8,128)(2,1)}, bf16[272,512]{1,0:T(8,128)(2,1)}, bf16[272,512]{1,0:T(8,128)(2,1)}, bf16[272,512]{1,0:T(8,128)(2,1)}, bf16[4352,5...) custom-call(s32[16]{0:T(128)} %pad_add_fusion.1.spans, s32[2]{0:T(128)} %pad_add_fusion.meta, bf16[256,512]{1,0:T(8,128)(2,1)} %copy-done.9, ...), custom_call_target="tpu_custom_call" | custom-call | flops 9126805504 | bytes 8912896 | tf_op jit(solution)/shard_map/attend/pallas_call | solution.py:232
  50.5 0.1 collective-permute-start.7
  50.6 0.1 collective-permute-start.8
  50.6 0.0 collective-permute-done.10.refs_0_
  50.7 3.4 %collective-permute-start.9 = (bf16[272,512]{1,0:T(8,128)(2,1)}, bf16[272,512]{1,0:T(8,128)(2,1)S(1)}, u32[]{:S(2)}, u32[]{:S(2)}) collective-permute-start(bf16[272,512]{1,0:T(8,128)(2,1)} %get-tuple-element.34), channel_id=1, source_target_pairs={{0,24},{4,28},{8,16},{12,20},{16,8},{20,12},{24,0},{28,4},{1,25},{... | collective-permute-start | bytes 835592 | tf_op jit(solution)/shard_map/ppermute | solution.py:372
  54.1 0.7 copy-done.15
  54.7 0.1 copy-done.17
  54.8 19.0 %attend.4 = (bf16[272,512]{1,0:T(8,128)(2,1)}, bf16[272,512]{1,0:T(8,128)(2,1)}, bf16[272,512]{1,0:T(8,128)(2,1)}) custom-call(s32[16]{0:T(128)} %pad_add_fusion.1.spans, s32[2]{0:T(128)} %pad_add_fusion.meta, bf16[256,512]{1,0:T(8,128)(2,1)} %copy-done.13, bf16[256,512]{1,0:T(8,128)(2,1)} %copy-done.15, bf16[256,512]{1,0:T(8,128)(2,1)} %copy-done.17, ...), custom_call_target="tpu_custom_call" | custom-call | flops 6845104128 | bytes 8912896 | tf_op jit(solution)/shard_map/attend/pallas_call | solution.py:232
  73.9 0.0 collective-permute-start.17
  73.9 0.0 collective-permute-done.7.refs_1_
  73.9 0.0 collective-permute-done.9.refs_3_
  73.9 0.7 copy-done.6
  74.6 0.1 copy-done.7
  74.7 0.1 copy-done.8
  74.8 2.5 %merge.2 = (bf16[128,512]{1,0:T(8,128)(2,1)}, bf16[128,512]{1,0:T(8,128)(2,1)}) custom-call(bf16[272,512]{1,0:T(8,128)(2,1)} %get-tuple-element.31.refs_0_, bf16[272,512]{1,0:T(8,128)(2,1)} %copy-done.6, bf16[272,512]{1,0:T(8,128)(2,1)} %copy-done.7, bf16[272,512]{1,0:T(8,128)(2,1)} %copy-done.8, bf16[272,512]{1,0:T(8,128)(2,1)} %get-tuple-element.38.refs_4_), custom_call_target="tpu_custom_call" | custom-call | bytes 1048576 | tf_op jit(solution)/shard_map/merge/pallas_call | solution.py:292
  77.3 3.5 %collective-permute-start.19 = (bf16[272,512]{1,0:T(8,128)(2,1)}, bf16[272,512]{1,0:T(8,128)(2,1)S(1)}, u32[]{:S(2)}, u32[]{:S(2)}) collective-permute-start(bf16[272,512]{1,0:T(8,128)(2,1)} %get-tuple-element.46), channel_id=1, source_target_pairs={{0,24},{4,28},{8,16},{12,20},{16,8},{20,12},{24,0},{28,4},{1,25},{... | collective-permute-start | bytes 835592 | tf_op jit(solution)/shard_map/ppermute | solution.py:372
  80.8 0.7 copy-done.10
  81.4 6.7 %project.2 = (bf16[128,1024]{1,0:T(8,128)(2,1)}, bf16[128,1024]{1,0:T(8,128)(2,1)}, bf16[128,1024]{1,0:T(8,128)(2,1)}, f32[128,1024]{1,0:T(8,128)}) custom-call(s32[2]{0:T(128)} %pad_add_fusion.meta, bf16[128,512]{1,0:T(8,128)(2,1)} %get-tuple-element.39.keep, bf16[128,512]{1,0:T(8,128)(2,1)} %copy-done.10, bf16[1024,4096]{1,0:T(8,128)(2,1)} %refs_3_.3, ...), custom_call_target="tpu_custom_call" | custom-call | flops 1073741824 | bytes 8388608 | tf_op jit(solution)/shard_map/project/pallas_call | solution.py:338
  88.2 1.6 %collective-permute-start.16 = (bf16[128,1024]{1,0:T(8,128)(2,1)}, bf16[128,1024]{1,0:T(8,128)(2,1)S(1)}, u32[]{:S(2)}, u32[]{:S(2)}) collective-permute-start(bf16[128,1024]{1,0:T(8,128)(2,1)} %get-tuple-element.44), channel_id=1, source_target_pairs={{0,1},{1,0},{2,3},{3,2},{4,5},{5,4},{6,7},{7,6},{8,9},{9,8},{10,11... | collective-permute-start | bytes 786440 | tf_op jit(solution)/shard_map/ppermute | solution.py:372
  89.7 2.6 %collective-permute-start.15 = (bf16[128,1024]{1,0:T(8,128)(2,1)}, bf16[128,1024]{1,0:T(8,128)(2,1)S(1)}, u32[]{:S(2)}, u32[]{:S(2)}) collective-permute-start(bf16[128,1024]{1,0:T(8,128)(2,1)} %get-tuple-element.43), channel_id=1, source_target_pairs={{0,2},{1,3},{2,0},{3,1},{4,6},{5,7},{6,4},{7,5},{8,10},{9,11},{10,... | collective-permute-start | bytes 786440 | tf_op jit(solution)/shard_map/ppermute | solution.py:372
  92.3 0.0 collective-permute-done.17.refs_1_
  92.3 0.3 collective-permute-start.14
  92.5 11.8 %attend.5.refs_0_ = bf16[272,512]{1,0:T(8,128)(2,1)} custom-call(s32[16]{0:T(128)} %pad_add_fusion.1.spans, s32[2]{0:T(128)} %pad_add_fusion.meta, bf16[256,512]{1,0:T(8,128)(2,1)} %copy-done, bf16[4352,512]{1,0:T(8,128)(2,1)} %get-tuple-element.36.refs_3_.refs_1_, bf16[4352,512]{1,0:T(8,128)(2,1)} %get-tuple-element.37.refs_4_.refs_2_, ...), custom_call_target="tpu_custom_call" | custom-call | flops 2281701376 | bytes 8912896 | tf_op jit(solution)/shard_map/attend/pallas_call | solution.py:232
  104.3 0.0 collective-permute-done.18.refs_2_
  104.4 0.7 copy-done.4
  105.1 0.7 copy-done.5
  105.8 2.5 %merge.3 = (bf16[128,512]{1,0:T(8,128)(2,1)}, bf16[128,512]{1,0:T(8,128)(2,1)}) custom-call(bf16[272,512]{1,0:T(8,128)(2,1)} %attend.5.refs_0_, bf16[272,512]{1,0:T(8,128)(2,1)} %copy-done.3, bf16[272,512]{1,0:T(8,128)(2,1)} %copy-done.4, bf16[272,512]{1,0:T(8,128)(2,1)} %copy-done.5), custom_call_target="tpu_custom_call" | custom-call | bytes 1048576 | tf_op jit(solution)/shard_map/merge/pallas_call | solution.py:292
  108.3 1.6 %collective-permute-done.20.got = bf16[128,512]{1,0:T(8,128)(2,1)S(1)} collective-permute-done((bf16[128,512]{1,0:T(8,128)(2,1)}, bf16[128,512]{1,0:T(8,128)(2,1)S(1)}, u32[]{:S(2)}, u32[]{:S(2)}) %collective-permute-start.20) | collective-permute-done | bytes 131104 | tf_op jit(solution)/shard_map/ppermute | solution.py:372
  109.8 0.6 copy-done.11
  110.5 6.9 %project.3 = (bf16[128,1024]{1,0:T(8,128)(2,1)}, bf16[128,1024]{1,0:T(8,128)(2,1)}, bf16[128,1024]{1,0:T(8,128)(2,1)}, f32[128,1024]{1,0:T(8,128)}) custom-call(s32[2]{0:T(128)} %pad_add_fusion.meta, bf16[128,512]{1,0:T(8,128)(2,1)} %get-tuple-element.47.keep, bf16[128,512]{1,0:T(8,128)(2,1)} %copy-done.11, bf16[1024,4096]{1,0:T(8,128)(2,1)} %refs_3_.3, ...), custom_call_target="tpu_custom_call" | custom-call | flops 1073741824 | bytes 8388608 | tf_op jit(solution)/shard_map/project/pallas_call | solution.py:338
  117.4 0.7 collective-permute-start.23
  118.0 3.5 %collective-permute-start.22 = (bf16[128,1024]{1,0:T(8,128)(2,1)}, bf16[128,1024]{1,0:T(8,128)(2,1)S(1)}, u32[]{:S(2)}, u32[]{:S(2)}) collective-permute-start(bf16[128,1024]{1,0:T(8,128)(2,1)} %get-tuple-element.51), channel_id=1, source_target_pairs={{0,2},{1,3},{2,0},{3,1},{4,6},{5,7},{6,4},{7,5},{8,10},{9,11},{10,... | collective-permute-start | bytes 786440 | tf_op jit(solution)/shard_map/ppermute | solution.py:372
  121.5 0.3 collective-permute-start.21
  121.8 0.0 collective-permute-done.15
  121.8 0.0 collective-permute-done.14
  121.8 0.1 convert_add_fusion.1
  121.9 9.1 %collective-permute-done.23 = bf16[128,1024]{1,0:T(8,128)(2,1)S(1)} collective-permute-done((bf16[128,1024]{1,0:T(8,128)(2,1)}, bf16[128,1024]{1,0:T(8,128)(2,1)S(1)}, u32[]{:S(2)}, u32[]{:S(2)}) %collective-permute-start.23) | collective-permute-done | bytes 262176 | tf_op jit(solution)/shard_map/ppermute | solution.py:372
  131.0 9.1 %collective-permute-done.22 = bf16[128,1024]{1,0:T(8,128)(2,1)S(1)} collective-permute-done((bf16[128,1024]{1,0:T(8,128)(2,1)}, bf16[128,1024]{1,0:T(8,128)(2,1)S(1)}, u32[]{:S(2)}, u32[]{:S(2)}) %collective-permute-start.22) | collective-permute-done | bytes 262176 | tf_op jit(solution)/shard_map/ppermute | solution.py:372
  140.1 1.2 convert_add_fusion
  141.3 1.0 pad_maximum_fusion
  (41 shorter events, 0.1 us)
Async XLA Ops:
  1.0 1.7 %collective-permute-start.1 = (bf16[256,512]{1,0:T(8,128)(2,1)S(1)}, bf16[256,512]{1,0:T(8,128)(2,1)S(1)}, u32[]{:S(2)}, u32[]{:S(2)}) collective-permute-start(bf16[256,512]{1,0:T(8,128)(2,1)S(1)} %constant_dynamic-slice_fusion.3), channel_id=1, source_target_pairs={{0,4},{4,0},{8,12},{12,8},{16,20},{20,16},{24,28},{28,24},{1,5},{5... | collective-permute-start | bytes 786440 | tf_op jit(solution)/shard_map/ppermute | solution.py:372
  1.5 4.8 %copy-start.1 = (bf16[2048,1024]{1,0:T(8,128)(2,1)S(1)}, bf16[2048,1024]{1,0:T(8,128)(2,1)}, u32[]{:S(2)}) copy-start(bf16[2048,1024]{1,0:T(8,128)(2,1)} %refs_4_.1) | copy-start | bytes 12582916
  2.7 8.7 %copy-start.9 = (bf16[256,512]{1,0:T(8,128)(2,1)}, bf16[256,512]{1,0:T(8,128)(2,1)S(1)}, u32[]{:S(2)}) copy-start(bf16[256,512]{1,0:T(8,128)(2,1)S(1)} %pad_maximum_fusion.1.refs_0_) | copy-start | bytes 786436
  2.7 4.2 %copy-start.18 = (s32[8]{0:T(128)S(1)}, s32[8]{0:T(128)}, u32[]{:S(2)}) copy-start(s32[8]{0:T(128)} %param.8) | copy-start | bytes 100
  6.1 9.1 %collective-permute-start.6 = (bf16[2048,512]{1,0:T(8,128)(2,1)}, bf16[2048,512]{1,0:T(8,128)(2,1)}, u32[]{:S(2)}, u32[]{:S(2)}) collective-permute-start(bf16[2048,512]{1,0:T(8,128)(2,1)} %constant_dynamic-slice_fusion.1), channel_id=1, source_target_pairs={{0,4},{4,0},{8,12},{12,8},{16,20},{20,16},{24,28},{28,24},{1,5},{5... | collective-permute-start | bytes 6291464 | tf_op jit(solution)/shard_map/ppermute | solution.py:372
  6.5 18.4 %collective-permute-start.5 = (bf16[2048,512]{1,0:T(8,128)(2,1)S(1)}, bf16[2048,512]{1,0:T(8,128)(2,1)}, u32[]{:S(2)}, u32[]{:S(2)}) collective-permute-start(bf16[2048,512]{1,0:T(8,128)(2,1)S(1)} %constant_dynamic-slice_fusion.2), channel_id=1, source_target_pairs={{0,4},{4,0},{8,12},{12,8},{16,20},{20,16},{24,28},{28,24},{1,5},{5... | collective-permute-start | bytes 6291464 | tf_op jit(solution)/shard_map/ppermute | solution.py:372
  6.9 4.5 %collective-permute-start = (s32[8]{0:T(128)S(1)}, s32[8]{0:T(128)S(1)}, u32[]{:S(2)}, u32[]{:S(2)}) collective-permute-start(s32[8]{0:T(128)S(1)} %copy-done.18), channel_id=1, source_target_pairs={{0,4},{4,0},{8,12},{12,8},{16,20},{20,16},{24,28},{28,24},{1,5},{5... | collective-permute-start | bytes 104 | tf_op jit(solution)/shard_map/ppermute | solution.py:372
  7.1 9.9 %collective-permute-start.2 = (bf16[256,512]{1,0:T(8,128)(2,1)S(1)}, bf16[256,512]{1,0:T(8,128)(2,1)S(1)}, u32[]{:S(2)}, u32[]{:S(2)}) collective-permute-start(bf16[256,512]{1,0:T(8,128)(2,1)S(1)} %pad_maximum_fusion.1.refs_0_), channel_id=1, source_target_pairs={{0,8},{4,12},{8,0},{12,4},{16,24},{20,28},{24,16},{28,20},{1,9},{5... | collective-permute-start | bytes 786440 | tf_op jit(solution)/shard_map/ppermute | solution.py:372
  9.9 13.8 %collective-permute-start.3 = (bf16[256,512]{1,0:T(8,128)(2,1)S(1)}, bf16[256,512]{1,0:T(8,128)(2,1)S(1)}, u32[]{:S(2)}, u32[]{:S(2)}) collective-permute-start(bf16[256,512]{1,0:T(8,128)(2,1)S(1)} %pad_maximum_fusion.1.refs_0_), channel_id=1, source_target_pairs={{0,16},{4,20},{8,24},{12,28},{16,0},{20,4},{24,8},{28,12},{1,17},{... | collective-permute-start | bytes 786440 | tf_op jit(solution)/shard_map/ppermute | solution.py:372
  11.4 13.6 %collective-permute-start.4 = (bf16[256,512]{1,0:T(8,128)(2,1)S(1)}, bf16[256,512]{1,0:T(8,128)(2,1)S(1)}, u32[]{:S(2)}, u32[]{:S(2)}) collective-permute-start(bf16[256,512]{1,0:T(8,128)(2,1)S(1)} %pad_maximum_fusion.1.refs_0_), channel_id=1, source_target_pairs={{0,24},{4,28},{8,16},{12,20},{16,8},{20,12},{24,0},{28,4},{1,25},{... | collective-permute-start | bytes 786440 | tf_op jit(solution)/shard_map/ppermute | solution.py:372
  15.2 35.3 %copy-start = (bf16[256,512]{1,0:T(8,128)(2,1)}, bf16[256,512]{1,0:T(8,128)(2,1)S(1)}, u32[]{:S(2)}) copy-start(bf16[256,512]{1,0:T(8,128)(2,1)S(1)} %pad_maximum_fusion.2.refs_0_) | copy-start | bytes 786436
  15.2 35.5 %collective-permute-start.10 = (bf16[256,512]{1,0:T(8,128)(2,1)S(1)}, bf16[256,512]{1,0:T(8,128)(2,1)S(1)}, u32[]{:S(2)}, u32[]{:S(2)}) collective-permute-start(bf16[256,512]{1,0:T(8,128)(2,1)S(1)} %pad_maximum_fusion.2.refs_0_), channel_id=1, source_target_pairs={{0,8},{4,12},{8,0},{12,4},{16,24},{20,28},{24,16},{28,20},{1,9},{5... | collective-permute-start | bytes 786440 | tf_op jit(solution)/shard_map/ppermute | solution.py:372
  17.0 8.0 %copy-start.12 = (bf16[256,512]{1,0:T(8,128)(2,1)}, bf16[256,512]{1,0:T(8,128)(2,1)S(1)}, u32[]{:S(2)}) copy-start(bf16[256,512]{1,0:T(8,128)(2,1)S(1)} %collective-permute-done.2.refs_1_) | copy-start | bytes 786436
  17.0 37.1 %collective-permute-start.11 = (bf16[256,512]{1,0:T(8,128)(2,1)S(1)}, bf16[256,512]{1,0:T(8,128)(2,1)S(1)}, u32[]{:S(2)}, u32[]{:S(2)}) collective-permute-start(bf16[256,512]{1,0:T(8,128)(2,1)S(1)} %pad_maximum_fusion.2.refs_0_), channel_id=1, source_target_pairs={{0,16},{4,20},{8,24},{12,28},{16,0},{20,4},{24,8},{28,12},{1,17},{... | collective-permute-start | bytes 786440 | tf_op jit(solution)/shard_map/ppermute | solution.py:372
  23.7 1.3 copy-start.14
  23.7 30.3 %collective-permute-start.12 = (bf16[256,512]{1,0:T(8,128)(2,1)S(1)}, bf16[256,512]{1,0:T(8,128)(2,1)S(1)}, u32[]{:S(2)}, u32[]{:S(2)}) collective-permute-start(bf16[256,512]{1,0:T(8,128)(2,1)S(1)} %pad_maximum_fusion.2.refs_0_), channel_id=1, source_target_pairs={{0,24},{4,28},{8,16},{12,20},{16,8},{20,12},{24,0},{28,4},{1,25},{... | collective-permute-start | bytes 786440 | tf_op jit(solution)/shard_map/ppermute | solution.py:372
  25.0 0.7 copy-start.16
  50.5 23.4 %collective-permute-start.7 = (bf16[272,512]{1,0:T(8,128)(2,1)}, bf16[272,512]{1,0:T(8,128)(2,1)S(1)}, u32[]{:S(2)}, u32[]{:S(2)}) collective-permute-start(bf16[272,512]{1,0:T(8,128)(2,1)} %get-tuple-element.32), channel_id=1, source_target_pairs={{0,8},{4,12},{8,0},{12,4},{16,24},{20,28},{24,16},{28,20},{1,9},{5... | collective-permute-start | bytes 835592 | tf_op jit(solution)/shard_map/ppermute | solution.py:372
  50.6 23.3 %collective-permute-start.8 = (bf16[272,512]{1,0:T(8,128)(2,1)}, bf16[272,512]{1,0:T(8,128)(2,1)S(1)}, u32[]{:S(2)}, u32[]{:S(2)}) collective-permute-start(bf16[272,512]{1,0:T(8,128)(2,1)} %get-tuple-element.33), channel_id=1, source_target_pairs={{0,16},{4,20},{8,24},{12,28},{16,0},{20,4},{24,8},{28,12},{1,17},{... | collective-permute-start | bytes 835592 | tf_op jit(solution)/shard_map/ppermute | solution.py:372
  50.6 3.4 %copy-start.13 = (bf16[256,512]{1,0:T(8,128)(2,1)}, bf16[256,512]{1,0:T(8,128)(2,1)S(1)}, u32[]{:S(2)}) copy-start(bf16[256,512]{1,0:T(8,128)(2,1)S(1)} %collective-permute-done.10.refs_0_) | copy-start | bytes 786436
  50.7 23.2 %collective-permute-start.9 = (bf16[272,512]{1,0:T(8,128)(2,1)}, bf16[272,512]{1,0:T(8,128)(2,1)S(1)}, u32[]{:S(2)}, u32[]{:S(2)}) collective-permute-start(bf16[272,512]{1,0:T(8,128)(2,1)} %get-tuple-element.34), channel_id=1, source_target_pairs={{0,24},{4,28},{8,16},{12,20},{16,8},{20,12},{24,0},{28,4},{1,25},{... | collective-permute-start | bytes 835592 | tf_op jit(solution)/shard_map/ppermute | solution.py:372
  54.0 0.7 copy-start.15
  54.1 0.8 copy-start.17
  73.9 18.4 %collective-permute-start.17 = (bf16[272,512]{1,0:T(8,128)(2,1)}, bf16[272,512]{1,0:T(8,128)(2,1)S(1)}, u32[]{:S(2)}, u32[]{:S(2)}) collective-permute-start(bf16[272,512]{1,0:T(8,128)(2,1)} %get-tuple-element.38.refs_4_), channel_id=1, source_target_pairs={{0,8},{4,12},{8,0},{12,4},{16,24},{20,28},{24,16},{28,20},{1,9},{5... | collective-permute-start | bytes 835592 | tf_op jit(solution)/shard_map/ppermute | solution.py:372
  73.9 0.7 copy-start.6
  73.9 0.8 copy-start.7
  73.9 0.9 copy-start.8
  77.3 3.5 %collective-permute-start.13 = (bf16[128,512]{1,0:T(8,128)(2,1)}, bf16[128,512]{1,0:T(8,128)(2,1)S(1)}, u32[]{:S(2)}, u32[]{:S(2)}) collective-permute-start(bf16[128,512]{1,0:T(8,128)(2,1)} %get-tuple-element.40), channel_id=1, source_target_pairs={{0,4},{4,0},{8,12},{12,8},{16,20},{20,16},{24,28},{28,24},{1,5},{5... | collective-permute-start | bytes 393224 | tf_op jit(solution)/shard_map/ppermute | solution.py:372
  77.3 27.0 %collective-permute-start.18 = (bf16[272,512]{1,0:T(8,128)(2,1)}, bf16[272,512]{1,0:T(8,128)(2,1)S(1)}, u32[]{:S(2)}, u32[]{:S(2)}) collective-permute-start(bf16[272,512]{1,0:T(8,128)(2,1)} %get-tuple-element.45), channel_id=1, source_target_pairs={{0,16},{4,20},{8,24},{12,28},{16,0},{20,4},{24,8},{28,12},{1,17},{... | collective-permute-start | bytes 835592 | tf_op jit(solution)/shard_map/ppermute | solution.py:372
  77.3 27.1 %collective-permute-start.19 = (bf16[272,512]{1,0:T(8,128)(2,1)}, bf16[272,512]{1,0:T(8,128)(2,1)S(1)}, u32[]{:S(2)}, u32[]{:S(2)}) collective-permute-start(bf16[272,512]{1,0:T(8,128)(2,1)} %get-tuple-element.46), channel_id=1, source_target_pairs={{0,24},{4,28},{8,16},{12,20},{16,8},{20,12},{24,0},{28,4},{1,25},{... | collective-permute-start | bytes 835592 | tf_op jit(solution)/shard_map/ppermute | solution.py:372
  80.8 0.7 copy-start.10
  88.2 33.4 %collective-permute-start.16 = (bf16[128,1024]{1,0:T(8,128)(2,1)}, bf16[128,1024]{1,0:T(8,128)(2,1)S(1)}, u32[]{:S(2)}, u32[]{:S(2)}) collective-permute-start(bf16[128,1024]{1,0:T(8,128)(2,1)} %get-tuple-element.44), channel_id=1, source_target_pairs={{0,1},{1,0},{2,3},{3,2},{4,5},{5,4},{6,7},{7,6},{8,9},{9,8},{10,11... | collective-permute-start | bytes 786440 | tf_op jit(solution)/shard_map/ppermute | solution.py:372
  89.7 32.0 %collective-permute-start.15 = (bf16[128,1024]{1,0:T(8,128)(2,1)}, bf16[128,1024]{1,0:T(8,128)(2,1)S(1)}, u32[]{:S(2)}, u32[]{:S(2)}) collective-permute-start(bf16[128,1024]{1,0:T(8,128)(2,1)} %get-tuple-element.43), channel_id=1, source_target_pairs={{0,2},{1,3},{2,0},{3,1},{4,6},{5,7},{6,4},{7,5},{8,10},{9,11},{10,... | collective-permute-start | bytes 786440 | tf_op jit(solution)/shard_map/ppermute | solution.py:372
  92.3 12.0 %copy-start.3 = (bf16[272,512]{1,0:T(8,128)(2,1)}, bf16[272,512]{1,0:T(8,128)(2,1)S(1)}, u32[]{:S(2)}) copy-start(bf16[272,512]{1,0:T(8,128)(2,1)S(1)} %collective-permute-done.17.refs_1_) | copy-start | bytes 835588
  92.3 29.5 %collective-permute-start.14 = (bf16[128,1024]{1,0:T(8,128)(2,1)}, bf16[128,1024]{1,0:T(8,128)(2,1)S(1)}, u32[]{:S(2)}, u32[]{:S(2)}) collective-permute-start(bf16[128,1024]{1,0:T(8,128)(2,1)} %get-tuple-element.42.refs_3_), channel_id=1, source_target_pairs={{0,3},{1,2},{2,1},{3,0},{4,7},{5,6},{6,5},{7,4},{8,11},{9,10},{10,... | collective-permute-start | bytes 786440 | tf_op jit(solution)/shard_map/ppermute | solution.py:372
  104.3 0.7 copy-start.4
  105.1 0.7 copy-start.5
  108.3 1.6 %collective-permute-start.20 = (bf16[128,512]{1,0:T(8,128)(2,1)}, bf16[128,512]{1,0:T(8,128)(2,1)S(1)}, u32[]{:S(2)}, u32[]{:S(2)}) collective-permute-start(bf16[128,512]{1,0:T(8,128)(2,1)} %get-tuple-element.48), channel_id=1, source_target_pairs={{0,4},{4,0},{8,12},{12,8},{16,20},{20,16},{24,28},{28,24},{1,5},{5... | collective-permute-start | bytes 393224 | tf_op jit(solution)/shard_map/ppermute | solution.py:372
  109.8 0.7 copy-start.11
  110.5 11.3 %copy-start.2 = (f32[128,1024]{1,0:T(8,128)S(1)}, f32[128,1024]{1,0:T(8,128)}, u32[]{:S(2)}) copy-start(f32[128,1024]{1,0:T(8,128)} %get-tuple-element.41) | copy-start | bytes 1572868
  117.4 13.7 %collective-permute-start.23 = (bf16[128,1024]{1,0:T(8,128)(2,1)}, bf16[128,1024]{1,0:T(8,128)(2,1)S(1)}, u32[]{:S(2)}, u32[]{:S(2)}) collective-permute-start(bf16[128,1024]{1,0:T(8,128)(2,1)} %get-tuple-element.52), channel_id=1, source_target_pairs={{0,1},{1,0},{2,3},{3,2},{4,5},{5,4},{6,7},{7,6},{8,9},{9,8},{10,11... | collective-permute-start | bytes 786440 | tf_op jit(solution)/shard_map/ppermute | solution.py:372
  118.0 22.1 %collective-permute-start.22 = (bf16[128,1024]{1,0:T(8,128)(2,1)}, bf16[128,1024]{1,0:T(8,128)(2,1)S(1)}, u32[]{:S(2)}, u32[]{:S(2)}) collective-permute-start(bf16[128,1024]{1,0:T(8,128)(2,1)} %get-tuple-element.51), channel_id=1, source_target_pairs={{0,2},{1,3},{2,0},{3,1},{4,6},{5,7},{6,4},{7,5},{8,10},{9,11},{10,... | collective-permute-start | bytes 786440 | tf_op jit(solution)/shard_map/ppermute | solution.py:372
  121.5 18.6 %collective-permute-start.21 = (bf16[128,1024]{1,0:T(8,128)(2,1)}, bf16[128,1024]{1,0:T(8,128)(2,1)S(1)}, u32[]{:S(2)}, u32[]{:S(2)}) collective-permute-start(bf16[128,1024]{1,0:T(8,128)(2,1)} %get-tuple-element.50), channel_id=1, source_target_pairs={{0,3},{1,2},{2,1},{3,0},{4,7},{5,6},{6,5},{7,4},{8,11},{9,10},{10,... | collective-permute-start | bytes 786440 | tf_op jit(solution)/shard_map/ppermute | solution.py:372

commit v3 on v2

--- a/solution.py
+++ b/solution.py
@@ -12,13 +12,16 @@
 SPAN = 256
 STEP = 16
 UNIT = 256
-BLOCK = 4 * UNIT
+BLOCKS = (8 * UNIT, 2 * UNIT, UNIT)
 SUB = 256
+FIRST = 8
 SCALE = math.log2(math.e) / math.sqrt(HD)
 NT = (((1,), (1,)), ((), ()))
 NN = (((1,), (0,)), ((), ()))
 MIB = 2**20
-VMEM = 58 * MIB
+VMEM = 46 * MIB
+MERGE_VMEM = 12 * MIB
+PROJECT_VMEM = 16 * MIB
 
 
 def groups_of(rows):
@@ -31,6 +34,10 @@
 
 def stat_rows(rows):
     return (3 * len(groups_of(rows)) + 15) // 16 * 16
+
+
+def block_rows(tall):
+    return next(rows for rows in range(32, tall, 32) if rows + stat_rows(rows) == tall)
 
 
 def eye_of(size):
@@ -96,15 +103,15 @@
     if first:
         k_ref, v_ref = take(2)
     q_all, m_ref, s_even, s_odd, top_even, top_odd, acc = refs
-    rows = q_refs[0].shape[0]
+    starts, total = [], 0
+    for q_ref in q_refs:
+        starts.append(total)
+        total += q_ref.shape[0]
     step = pl.program_id(0)
     passages = (k_ref.shape[0] - UNIT) // SPAN
     count = sum(round_up(spans[i]) for i in range(passages))
-    units = (count + UNIT - 1) // UNIT
-    turns = units // (BLOCK // UNIT)
-    rest = units - turns * (BLOCK // UNIT)
-    total = blocks * rows
-    sub = min(SUB, total)
+    count = (count + UNIT - 1) // UNIT * UNIT
+    parts = [pl.ds(r, min(SUB, total - r)) for r in range(0, total, SUB)]
 
     def score(at, scores, top, part):
         s = lax.dot_general(
@@ -145,35 +152,37 @@
             if first:
                 pack(spans, own_k, got_k, k_ref, True)
             top_now[...] = jnp.full(top_now.shape, -3e38, jnp.float32)
-            for b in range(blocks):
-                q_all[b * rows : (b + 1) * rows, :] = q_refs[b][...]
+            for start, q_ref in zip(starts, q_refs):
+                q_all[start : start + q_ref.shape[0], :] = q_ref[...]
 
         def body(start, size):
             at = pl.ds(pl.multiple_of(start, UNIT), size)
-            for r in range(total // sub):
-                part = pl.ds(r * sub, sub)
+            for part in parts:
                 if now is not None:
                     score(at, scores_now, top_now, part)
                 if then is not None:
                     weigh(at, scores_then, top_then, part)
 
-        @pl.loop(0, turns)
-        def _(turn):
-            body(turn * BLOCK, BLOCK)
-
-        @pl.loop(0, rest)
-        def _(turn):
-            body(turns * BLOCK + turn * UNIT, UNIT)
+        start = jnp.int32(0)
+        for size in BLOCKS:
+            turns = (count - start) // size
+
+            @pl.loop(0, turns)
+            def _(turn, start=start, size=size):
+                body(start + turn * size, size)
+
+            start = start + turns * size
 
         if then is not None:
             for b in range(blocks):
                 finish(b, top_then)
 
     def finish(b, top):
+        rows = q_refs[b].shape[0]
         index = lax.broadcasted_iota(jnp.int32, (stat_rows(rows), HD), 0)
         packed = jnp.zeros(index.shape, jnp.float32)
         for u, (start, size) in enumerate(groups_of(rows)):
-            part = pl.ds(b * rows + start, size)
+            part = pl.ds(starts[b] + start, size)
             sums = acc[part, HD:]
             o_refs[b][start : start + size, :] = (acc[part, :HD] / sums).astype(jnp.bfloat16)
             logs = top[part, :] * SCALE + jnp.log2(sums)
@@ -211,17 +220,18 @@
 def attend(spans, meta, queries, raw, packed, after=()):
     first = packed is None
     blocks = len(queries)
-    rows, width = queries[0].shape
+    heights = [x.shape[0] for x in queries]
+    tall = [rows + stat_rows(rows) for rows in heights]
+    total = sum(heights)
+    width = queries[0].shape[1]
     heads = width // HD
-    tokens = raw[1].shape[0] if first else (packed[0].shape[0] - UNIT) // 2
+    tokens = raw[1].shape[0] if first else (packed[0].shape[1] - UNIT) // 2
     size = 2 * tokens + UNIT
-    tall = rows + stat_rows(rows)
     now = lambda t: jnp.minimum(t, heads - 1)
     then = lambda t: jnp.maximum(t - 1, 0)
-    total = blocks * rows
     packed_specs = [
-        pl.BlockSpec((size, HD), lambda t, n, m: (0, now(t))),
-        pl.BlockSpec((size, HD), lambda t, n, m: (0, then(t))),
+        pl.BlockSpec((None, size, HD), lambda t, n, m: (now(t), 0, 0)),
+        pl.BlockSpec((None, size, HD), lambda t, n, m: (then(t), 0, 0)),
     ]
     raw_specs = [
         pl.BlockSpec((tokens, HD), lambda t, n, m: (0, m[0] * heads + now(t))),
@@ -234,10 +244,10 @@
         grid_spec=pltpu.PrefetchScalarGridSpec(
             num_scalar_prefetch=2,
             grid=(heads + 1,),
-            in_specs=[pl.BlockSpec((rows, HD), lambda t, n, m: (0, now(t)))] * blocks
+            in_specs=[pl.BlockSpec((rows, HD), lambda t, n, m: (0, now(t))) for rows in heights]
             + (raw_specs if first else packed_specs)
             + [pl.BlockSpec(memory_space=pl.ANY)] * len(after),
-            out_specs=[pl.BlockSpec((tall, HD), lambda t, n, m: (0, then(t)))] * blocks
+            out_specs=[pl.BlockSpec((rows, HD), lambda t, n, m: (0, then(t))) for rows in tall]
             + (packed_specs if first else []),
             scratch_shapes=[
                 pltpu.VMEM((total, HD), jnp.bfloat16),
@@ -249,8 +259,8 @@
                 pltpu.VMEM((total, 2 * HD), jnp.float32),
             ],
         ),
-        out_shape=[jax.ShapeDtypeStruct((tall, width), jnp.bfloat16)] * blocks
-        + [jax.ShapeDtypeStruct((size, width), jnp.bfloat16)] * (2 if first else 0),
+        out_shape=[jax.ShapeDtypeStruct((rows, width), jnp.bfloat16) for rows in tall]
+        + [jax.ShapeDtypeStruct((heads, size, HD), jnp.bfloat16)] * (2 if first else 0),
         compiler_params=pltpu.CompilerParams(vmem_limit_bytes=VMEM),
         cost_estimate=pl.CostEstimate(
             flops=4 * total * size * width, bytes_accessed=4 * size * width, transcendentals=0
@@ -286,8 +296,9 @@
             out[there : there + size, cols] = merged.astype(jnp.bfloat16)
 
 
-def merge(parts, half, after=()):
+def merge(parts, after=()):
     width = parts[0].shape[1]
+    half = block_rows(parts[0].shape[0]) // 2
     shape = jax.ShapeDtypeStruct((half, width), jnp.bfloat16)
     return pl.pallas_call(
         functools.partial(merge_kernel, len(parts)),
@@ -295,7 +306,7 @@
         + [pl.BlockSpec(memory_space=pl.ANY)] * len(after),
         out_specs=[pl.BlockSpec(memory_space=pltpu.VMEM)] * 2,
         out_shape=[shape, shape],
-        compiler_params=pltpu.CompilerParams(vmem_limit_bytes=VMEM),
+        compiler_params=pltpu.CompilerParams(vmem_limit_bytes=MERGE_VMEM),
         cost_estimate=pl.CostEstimate(
             flops=0, bytes_accessed=4 * half * width * len(parts), transcendentals=0
         ),
@@ -303,61 +314,72 @@
     )(*parts, *after)
 
 
-def project_kernel(pieces, meta, keep, got, *refs):
-    weights, outs, attended = refs[:pieces], refs[pieces:-1], refs[-1]
-    step = pl.program_id(0)
+def project_kernel(meta, keep, got, weight, *refs):
+    groups = (len(refs) - 2) // 2
+    outs, made, attended, done = refs[:groups], refs[groups : 2 * groups], refs[-2], refs[-1]
     width = keep.shape[1]
-
-    @pl.when(step == 0)
-    def _():
-        attended[:, pl.ds(pl.multiple_of(meta[0] * width, HD), width)] = keep[...]
-        attended[:, pl.ds(pl.multiple_of((1 - meta[0]) * width, HD), width)] = got[...]
-
-    for i in range(len(outs)):
-
-        @pl.when(step == i)
-        def _(i=i):
-            deep = weights[0].shape[0]
-            outs[i][...] = sum(
-                lax.dot_general(
-                    attended[:, p * deep : (p + 1) * deep],
-                    weight[...],
-                    NN,
-                    preferred_element_type=jnp.float32,
-                )
-                for p, weight in enumerate(weights)
-            ).astype(outs[i].dtype)
+    cols = outs[0].shape[1]
+    attended[:, pl.ds(pl.multiple_of(meta[0] * width, HD), width)] = keep[...]
+    attended[:, pl.ds(pl.multiple_of((1 - meta[0]) * width, HD), width)] = got[...]
+    order = list(reversed(range(groups)))
+    copies = [pltpu.make_async_copy(made[d], outs[d], done.at[d]) for d in range(groups)]
+    for d in order:
+        at = pl.ds(pl.multiple_of((meta[1] ^ d) * cols, HD), cols)
+        made[d][...] = lax.dot_general(
+            attended[...], weight[:, at], NN, preferred_element_type=jnp.float32
+        ).astype(made[d].dtype)
+        copies[d].start()
+    for d in order:
+        copies[d].wait()
 
 
 def project(meta, keep, got, out_weight, groups):
     depth, total = out_weight.shape
     rows, width = keep.shape
     cols = total // groups
-    whole = pl.BlockSpec((rows, width), lambda t, m: (0, 0))
-    pieces = depth // UNIT
+    types = [jnp.float32] + [jnp.bfloat16] * (groups - 1)
     return pl.pallas_call(
-        functools.partial(project_kernel, pieces),
-        grid_spec=pltpu.PrefetchScalarGridSpec(
-            num_scalar_prefetch=1,
-            grid=(groups,),
-            in_specs=[whole, whole]
-            + [
-                pl.BlockSpec((UNIT, cols), lambda t, m, p=p: (p, m[1] ^ (groups - 1 - t)))
-                for p in range(pieces)
-            ],
-            out_specs=[pl.BlockSpec((rows, cols), lambda t, m: (0, 0))] * groups,
-            scratch_shapes=[pltpu.VMEM((rows, depth), jnp.bfloat16)],
-        ),
-        out_shape=[
-            jax.ShapeDtypeStruct((rows, cols), jnp.bfloat16 if t < groups - 1 else jnp.float32)
-            for t in range(groups)
-        ],
-        compiler_params=pltpu.CompilerParams(vmem_limit_bytes=VMEM),
+        project_kernel,
+        in_specs=[pl.BlockSpec(memory_space=pltpu.SMEM)]
+        + [pl.BlockSpec(memory_space=pltpu.VMEM)] * 3,
+        out_specs=[pl.BlockSpec(memory_space=pl.ANY)] * groups,
+        scratch_shapes=[pltpu.VMEM((rows, cols), kind) for kind in types]
+        + [pltpu.VMEM((rows, depth), jnp.bfloat16), pltpu.SemaphoreType.DMA((groups,))],
+        out_shape=[jax.ShapeDtypeStruct((rows, cols), kind) for kind in types],
+        compiler_params=pltpu.CompilerParams(vmem_limit_bytes=PROJECT_VMEM),
         cost_estimate=pl.CostEstimate(
             flops=2 * rows * depth * total, bytes_accessed=2 * depth * total, transcendentals=0
         ),
         name="project",
-    )(meta, keep, got, *[out_weight] * pieces)
+    )(meta, keep, got, out_weight)
+
+
+def total_kernel(count, *refs):
+    out = refs[-1]
+    out[...] = refs[0][...] + sum(ref[...].astype(jnp.float32) for ref in refs[1:count])
+
+
+def add_up(parts, start, total, before):
+    rows, cols = parts[0].shape
+    step = math.gcd(math.gcd(rows, start), 32)
+    return pl.pallas_call(
+        functools.partial(total_kernel, len(parts)),
+        grid=(rows // step,),
+        in_specs=[pl.BlockSpec((step, cols), lambda t: (t, 0))] * len(parts)
+        + [pl.BlockSpec(memory_space=pl.ANY)] * len(before),
+        out_specs=pl.BlockSpec((step, cols), lambda t: (start // step + t, 0)),
+        out_shape=jax.ShapeDtypeStruct((total, cols), jnp.float32),
+        input_output_aliases={len(parts): 0} if before else {},
+        compiler_params=pltpu.CompilerParams(vmem_limit_bytes=MERGE_VMEM),
+        cost_estimate=pl.CostEstimate(
+            flops=0, bytes_accessed=2 * rows * cols * (len(parts) + 3), transcendentals=0
+        ),
+        name="add_up",
+    )(*parts, *before)
+
+
+def first_rows(rows):
+    return (rows * FIRST // 16 + STEP - 1) // STEP * STEP
 
 
 def on_device(queries, keys, values, lengths, out_weight):
@@ -374,40 +396,42 @@
     def half(x, which):
         return lax.dynamic_slice(x, (0, which * width), (x.shape[0], width))
 
+    def others_of(x):
+        return [swap(x, k) for k in reversed(range(2, sources, 2))]
+
     def back_to_owners(blocks):
-        return [swap(block, 2 * i + 2) for i, block in enumerate(blocks)]
+        return [swap(block, k) for block, k in zip(blocks, reversed(range(2, sources, 2)))]
 
     def finish(parts, after=()):
-        keep, give = merge(parts, rows, after)
+        keep, give = merge(parts, after)
         return project(meta, keep, swap(give, 1), out_weight, groups)
 
-    def gather(blocks):
-        total = blocks[-1]
-        for d in range(groups - 1, 0, -1):
-            total = total + swap(blocks[groups - 1 - d], d, "head").astype(jnp.float32)
-        return total
-
-    rows = queries.shape[0] // 2
+    def arrive(blocks):
+        far = [swap(blocks[d], d, "head") for d in reversed(range(1, groups))]
+        return [blocks[0]] + far
+
+    rows = first_rows(queries.shape[0])
     mine = half(queries, core)
     theirs = swap(half(queries, 1 - core), 1)
-    ours = [jnp.concatenate([mine[:rows], theirs[:rows]]), jnp.concatenate([mine[rows:], theirs[rows:]])]
-    asked = [swap(ours[0], k) for k in range(2, sources, 2)]
-    keys_then, values_then, _ = lax.optimization_barrier((keys, values, ours[0]))
+    keys_then, values_then, _ = lax.optimization_barrier((keys, values, theirs))
     got_k = swap(half(keys_then, 1 - core), 1)
     got_v = swap(half(values_then, 1 - core), 1)
+    ours = [jnp.concatenate([mine[:rows], theirs[:rows]]), jnp.concatenate([mine[rows:], theirs[rows:]])]
+    asked = others_of(ours[0])
     spans = jnp.concatenate([lengths, swap(lengths, 1)])
-    ours[1], _ = lax.optimization_barrier((ours[1], got_v))
-    asked_then = [swap(ours[1], k) for k in range(2, sources, 2)]
+    late, _ = lax.optimization_barrier((ours[1], got_v))
+    asked_then = others_of(late)
 
     raw = (keys, got_k, values, got_v)
-    partial, packed = attend(spans, meta, [ours[0]] + asked, raw, None)
-    back = [partial[0]] + back_to_owners(partial[1:])
-    partial_then, _ = attend(spans, meta, asked_then, raw, packed)
+    own, packed = attend(spans, meta, ours, raw, None)
+    partial, _ = attend(spans, meta, asked, raw, packed)
+    back = back_to_owners(partial)
+    partial_then, _ = attend(spans, meta, asked_then, raw, packed, after=partial[:1])
     back_then = back_to_owners(partial_then)
-    blocks = finish(back, after=partial_then[:1])
-    partial_own, _ = attend(spans, meta, ours[1:], raw, packed, after=blocks[:1])
-    blocks_then = finish(partial_own + back_then)
-    return jnp.concatenate([gather(blocks), gather(blocks_then)], axis=0)
+    blocks = finish(own[:1] + back, after=partial_then[:1])
+    blocks_then = finish(own[1:] + back_then, after=blocks[:1])
+    out = add_up(arrive(blocks), 0, queries.shape[0], ())
+    return add_up(arrive(blocks_then), rows, queries.shape[0], (out,))
 
 
 def solution(mesh):

time: 143 us -> 128 us (0.90)
  Pallas kernels: 74.3 us -> 53.8 us
  starting transfers between devices: 27.8 us -> 34 us
  waiting for transfers between devices: 25.7 us -> 31.2 us
  other arithmetic: 3.69 us -> 0.19 us
  local copies, waits for them, and re-layouts: 10.7 us -> 8.09 us
    pallas_call x3, Pallas kernels: 55.6 us -> 44.3 us  [attend(): pl.pallas_call(functools.partial(attend_kernel, blocks, heads, first, len...]
    ppermute x24, starting transfers between devices: 27.8 us -> 34 us  [swap(): return lax.ppermute(x, axis, [(i, i ^ k) for i in range(n)])]
    ppermute x24, waiting for transfers between devices: 25.7 us -> 31.2 us  [swap(): return lax.ppermute(x, axis, [(i, i ^ k) for i in range(n)])]
    pallas_call x2 -> x4, Pallas kernels: 13.6 us -> 8.16 us  [the longest x2 5.34 us: project(): pl.pallas_call(project_kernel, in_specs=[pl.BlockSpec(memory_space=pltpu....]
    pallas_call x2, Pallas kernels: 5.05 us -> 1.35 us  [merge(): pl.pallas_call(functools.partial(merge_kernel, len(parts)), in_specs=[pl....]
    unnamed x38 -> x12, local copies, waits for them, and re-layouts: 5.03 us -> 2.28 us
  transfers between devices with their start and end apart: 24 -> 24, of which waited for: 5 -> 7; matrix products, arithmetic and copies ran while one was open for 2% -> 1% of each run, Pallas kernels for 52% -> 41%
where the time goes in v3:
time: 128 us; the launch traced here: 127 us
  Pallas kernels  53.8 us (42%)
  starting transfers between devices  34 us (27%)
  waiting for transfers between devices  31.2 us (24%)
  local copies, waits for them, and re-layouts  8.09 us (6%)
    pallas_call x3, Pallas kernels, attend(): pl.pallas_call(functools.partial(attend_kernel, blocks, heads, first, len...  44.3 us
    ppermute x24, starting transfers between devices, swap(): return lax.ppermute(x, axis, [(i, i ^ k) for i in range(n)])  34 us
    ppermute x24, waiting for transfers between devices, swap(): return lax.ppermute(x, axis, [(i, i ^ k) for i in range(n)])  31.2 us
    dynamic_slice x3, local copies, waits for them, and re-layouts, half(): return lax.dynamic_slice(x, (0, which * width), (x.shape[0], width))  5.78 us
    pallas_call x2, Pallas kernels, project(): pl.pallas_call(project_kernel, in_specs=[pl.BlockSpec(memory_space=pltpu....  5.34 us
    pallas_call x2, Pallas kernels, add_up(): pl.pallas_call(functools.partial(total_kernel, len(parts)), grid=(rows //...  2.82 us
  transfers between devices with their start and end apart: 24, of which 7 were waited for; matrix products, arithmetic and copies ran while one was open for 1% of the time, Pallas kernels for 41%

profile of v3, /device:TPU:0, one launch (start us, length us, event | category | flops | bytes accessed | tf_op | source)
XLA Modules:
  0.0 127.5 jit_solution(14150370049820253676)
XLA Ops:
  0.0 1.1 constant_dynamic-slice_fusion.3
  1.1 0.0 copy-start.3
  1.1 0.0 copy-start.2
  1.1 0.5 collective-permute-start.1
  1.7 1.2 collective-permute-done.1
  2.8 3.1 %constant_dynamic-slice_fusion.1 = bf16[2048,512]{1,0:T(8,128)(2,1)} fusion(bf16[2048,1024]{1,0:T(8,128)(2,1)} %refs_4_.1, s32[]{:T(128)S(6)} %select_n.9), kind=kLoop, calls=%fused_computation.3 | loop fusion | bytes 4194308 | tf_op jit(solution)/shard_map/dynamic_slice | solution.py:397
  5.9 0.4 collective-permute-start.3
  6.3 1.6 %constant_dynamic-slice_fusion.2 = bf16[2048,512]{1,0:T(8,128)(2,1)} fusion(bf16[2048,1024]{1,0:T(8,128)(2,1)S(1)} %copy-done.1, s32[]{:T(128)S(6)} %select_n.9), kind=kLoop, calls=%fused_computation.4 | loop fusion | bytes 4194308 | tf_op jit(solution)/shard_map/dynamic_slice | solution.py:397
  7.9 0.1 collective-permute-start.2
  8.0 0.4 collective-permute-start
  8.4 0.1 pad_add_fusion.meta
  8.5 1.6 %collective-permute-done = s32[8]{0:T(128)S(1)} collective-permute-done((s32[8]{0:T(128)S(1)}, s32[8]{0:T(128)S(1)}, u32[]{:S(2)}, u32[]{:S(2)}) %collective-permute-start) | collective-permute-done | bytes 64 | tf_op jit(solution)/shard_map/ppermute | solution.py:394
  10.1 0.1 pad_add_fusion.1.spans
  10.2 3.8 %collective-permute-start.7 = (bf16[256,512]{1,0:T(8,128)(2,1)S(1)}, bf16[256,512]{1,0:T(8,128)(2,1)S(1)}, u32[]{:S(2)}, u32[]{:S(2)}) collective-permute-start(bf16[256,512]{1,0:T(8,128)(2,1)S(1)} %pad_maximum_fusion.refs_0_), channel_id=1, source_target_pairs={{0,24},{4,28},{8,16},{12,20},{16,8},{20,12},{24,0},{28,4},{1,25},{... | collective-permute-start | bytes 786440 | tf_op jit(solution)/shard_map/ppermute | solution.py:394
  14.0 0.5 collective-permute-start.8
  14.5 0.1 collective-permute-start.9
  14.7 0.0 collective-permute-done.3.refs_5_
  14.7 2.9 %collective-permute-start.4 = (bf16[256,512]{1,0:T(8,128)(2,1)S(1)}, bf16[256,512]{1,0:T(8,128)(2,1)S(1)}, u32[]{:S(2)}, u32[]{:S(2)}) collective-permute-start(bf16[256,512]{1,0:T(8,128)(2,1)S(1)} %pad_maximum_fusion.1.refs_1_), channel_id=1, source_target_pairs={{0,24},{4,28},{8,16},{12,20},{16,8},{20,12},{24,0},{28,4},{1,25},{... | collective-permute-start | bytes 786440 | tf_op jit(solution)/shard_map/ppermute | solution.py:394
  17.6 0.0 collective-permute-done.2.refs_3_
  17.6 0.5 collective-permute-start.5
  18.1 14.7 %attend.3 = (bf16[272,512]{1,0:T(8,128)(2,1)S(1)}, bf16[272,512]{1,0:T(8,128)(2,1)S(1)}, bf16[4,4352,128]{2,1,0:T(8,128)(2,1)}, bf16[4,4352,128]{2,1,0:T(8,128)(2,1)}) custom-call(s32[16]{0:T(128)S(1)} %pad_add_fusion.1.spans, s32[2]{0:T(128)S(1)} %pad_add_fusion.meta, bf16[256,512]{1,0:T(8,128)(2,1)S(1)} %pad_maximum_fusion.refs_0_, ...), custom_call_target="tpu_custom_call" | custom-call | flops 4563402752 | bytes 8912896 | tf_op jit(solution)/shard_map/attend/pallas_call | solution.py:242
  32.8 0.0 collective-permute-done.7.refs_0_
  32.8 0.0 collective-permute-start.6
  32.8 0.0 collective-permute-done.8.refs_1_
  32.8 0.0 collective-permute-done.9.refs_2_
  32.9 2.3 %copy-done = bf16[4,4352,128]{2,1,0:T(8,128)(2,1)S(1)} copy-done((bf16[4,4352,128]{2,1,0:T(8,128)(2,1)S(1)}, bf16[4,4352,128]{2,1,0:T(8,128)(2,1)}, u32[]{:S(2)}) %copy-start) | copy-done | bytes 4456472
  35.1 14.5 %attend.4 = (bf16[272,512]{1,0:T(8,128)(2,1)S(1)}, bf16[272,512]{1,0:T(8,128)(2,1)S(1)}, bf16[272,512]{1,0:T(8,128)(2,1)S(1)}) custom-call(s32[16]{0:T(128)S(1)} %pad_add_fusion.1.spans, s32[2]{0:T(128)S(1)} %pad_add_fusion.meta, bf16[256,512]{1,0:T(8,128)(2,1)S(1)} %collective-permute-done.7.refs_0_, bf16[256,512]{1,0:T(8,128)(2,1)S(1)} %collective-permute-done.8.refs_1_, ...), custom_call_target="tpu_custom_call" | custom-call | flops 6845104128 | bytes 8912896 | tf_op jit(solution)/shard_map/attend/pallas_call | solution.py:242
  49.6 3.0 %collective-permute-start.13 = (bf16[272,512]{1,0:T(8,128)(2,1)S(1)}, bf16[272,512]{1,0:T(8,128)(2,1)S(1)}, u32[]{:S(2)}, u32[]{:S(2)}) collective-permute-start(bf16[272,512]{1,0:T(8,128)(2,1)S(1)} %get-tuple-element.36.refs_5_), channel_id=1, source_target_pairs={{0,24},{4,28},{8,16},{12,20},{16,8},{20,12},{24,0},{28,4},{1,25},{... | collective-permute-start | bytes 835592 | tf_op jit(solution)/shard_map/ppermute | solution.py:394
  52.6 0.0 collective-permute-start.14
  52.6 0.0 collective-permute-done.4.refs_0_
  52.6 0.0 slice-start.1
  52.6 1.0 collective-permute-start.15
  53.7 0.0 collective-permute-done.5.refs_1_
  53.7 0.0 collective-permute-done.6.refs_2_
  53.7 15.1 %attend.5 = (bf16[272,512]{1,0:T(8,128)(2,1)S(1)}, bf16[272,512]{1,0:T(8,128)(2,1)S(1)}, bf16[272,512]{1,0:T(8,128)(2,1)S(1)}) custom-call(s32[16]{0:T(128)S(1)} %pad_add_fusion.1.spans, s32[2]{0:T(128)S(1)} %pad_add_fusion.meta, bf16[256,512]{1,0:T(8,128)(2,1)S(1)} %collective-permute-done.4.refs_0_, bf16[256,512]{1,0:T(8,128)(2,1)S(1)} %collective-permute-done.5.refs_1_, ...), custom_call_target="tpu_custom_call" | custom-call | flops 6845104128 | bytes 8912896 | tf_op jit(solution)/shard_map/attend/pallas_call | solution.py:242
  68.8 2.5 %collective-permute-start.10 = (bf16[272,512]{1,0:T(8,128)(2,1)S(1)}, bf16[272,512]{1,0:T(8,128)(2,1)S(1)}, u32[]{:S(2)}, u32[]{:S(2)}) collective-permute-start(bf16[272,512]{1,0:T(8,128)(2,1)S(1)} %get-tuple-element.37.refs_4_), channel_id=1, source_target_pairs={{0,24},{4,28},{8,16},{12,20},{16,8},{20,12},{24,0},{28,4},{1,25},{... | collective-permute-start | bytes 835592 | tf_op jit(solution)/shard_map/ppermute | solution.py:394
  71.3 0.0 collective-permute-start.11
  71.3 0.0 collective-permute-done.13.refs_1_
  71.3 1.1 collective-permute-start.12
  72.3 0.0 collective-permute-done.14.refs_2_
  72.3 0.0 collective-permute-done.15.refs_3_
  72.3 0.7 merge.2
  73.0 0.1 collective-permute-start.16
  73.1 1.3 %collective-permute-done.16.got = bf16[128,512]{1,0:T(8,128)(2,1)S(1)} collective-permute-done((bf16[128,512]{1,0:T(8,128)(2,1)S(1)}, bf16[128,512]{1,0:T(8,128)(2,1)S(1)}, u32[]{:S(2)}, u32[]{:S(2)}) %collective-permute-start.16) | collective-permute-done | bytes 131104 | tf_op jit(solution)/shard_map/ppermute | solution.py:394
  74.5 2.8 %project.2 = (f32[128,1024]{1,0:T(8,128)S(1)}, bf16[128,1024]{1,0:T(8,128)(2,1)S(1)}, bf16[128,1024]{1,0:T(8,128)(2,1)S(1)}, bf16[128,1024]{1,0:T(8,128)(2,1)S(1)}) custom-call(s32[2]{0:T(128)S(1)} %pad_add_fusion.meta, bf16[128,512]{1,0:T(8,128)(2,1)S(1)} %get-tuple-element.43.keep, bf16[128,512]{1,0:T(8,128)(2,1)S(1)} %collective-permute-done.16.got, ...), custom_call_target="tpu_custom_call" | custom-call | flops 1073741824 | bytes 8388608 | tf_op jit(solution)/shard_map/project/pallas_call | solution.py:341
  77.2 3.7 %collective-permute-start.21 = (bf16[128,1024]{1,0:T(8,128)(2,1)S(1)}, bf16[128,1024]{1,0:T(8,128)(2,1)S(1)}, u32[]{:S(2)}, u32[]{:S(2)}) collective-permute-start(bf16[128,1024]{1,0:T(8,128)(2,1)S(1)} %get-tuple-element.52), channel_id=1, source_target_pairs={{0,3},{1,2},{2,1},{3,0},{4,7},{5,6},{6,5},{7,4},{8,11},{9,10},{10,... | collective-permute-start | bytes 786440 | tf_op jit(solution)/shard_map/ppermute | solution.py:394
  80.9 1.5 %collective-permute-done.11.refs_2_ = bf16[272,512]{1,0:T(8,128)(2,1)S(1)} collective-permute-done((bf16[272,512]{1,0:T(8,128)(2,1)S(1)}, bf16[272,512]{1,0:T(8,128)(2,1)S(1)}, u32[]{:S(2)}, u32[]{:S(2)}) %collective-permute-start.11) | collective-permute-done | bytes 278560 | tf_op jit(solution)/shard_map/ppermute | solution.py:394
  82.4 0.2 collective-permute-done.12.refs_3_
  82.6 0.7 merge.3
  83.3 0.1 collective-permute-start.17
  83.4 2.7 %collective-permute-start.22 = (bf16[128,1024]{1,0:T(8,128)(2,1)S(1)}, bf16[128,1024]{1,0:T(8,128)(2,1)S(1)}, u32[]{:S(2)}, u32[]{:S(2)}) collective-permute-start(bf16[128,1024]{1,0:T(8,128)(2,1)S(1)} %get-tuple-element.53), channel_id=1, source_target_pairs={{0,2},{1,3},{2,0},{3,1},{4,6},{5,7},{6,4},{7,5},{8,10},{9,11},{10,... | collective-permute-start | bytes 786440 | tf_op jit(solution)/shard_map/ppermute | solution.py:394
  86.1 1.6 %collective-permute-start.23 = (bf16[128,1024]{1,0:T(8,128)(2,1)S(1)}, bf16[128,1024]{1,0:T(8,128)(2,1)S(1)}, u32[]{:S(2)}, u32[]{:S(2)}) collective-permute-start(bf16[128,1024]{1,0:T(8,128)(2,1)S(1)} %get-tuple-element.54), channel_id=1, source_target_pairs={{0,1},{1,0},{2,3},{3,2},{4,5},{5,4},{6,7},{7,6},{8,9},{9,8},{10,11... | collective-permute-start | bytes 786440 | tf_op jit(solution)/shard_map/ppermute | solution.py:394
  87.6 2.5 %project.3 = (f32[128,1024]{1,0:T(8,128)S(1)}, bf16[128,1024]{1,0:T(8,128)(2,1)S(1)}, bf16[128,1024]{1,0:T(8,128)(2,1)S(1)}, bf16[128,1024]{1,0:T(8,128)(2,1)S(1)}) custom-call(s32[2]{0:T(128)S(1)} %pad_add_fusion.meta, bf16[128,512]{1,0:T(8,128)(2,1)S(1)} %get-tuple-element.46.keep, bf16[128,512]{1,0:T(8,128)(2,1)S(1)} %collective-permute-done.17.got, ...), custom_call_target="tpu_custom_call" | custom-call | flops 1073741824 | bytes 8388608 | tf_op jit(solution)/shard_map/project/pallas_call | solution.py:341
  90.2 0.8 collective-permute-start.18
  91.0 1.2 collective-permute-start.19
  92.2 0.0 collective-permute-done.21.refs_1_
  92.2 7.1 %collective-permute-start.20 = (bf16[128,1024]{1,0:T(8,128)(2,1)S(1)}, bf16[128,1024]{1,0:T(8,128)(2,1)S(1)}, u32[]{:S(2)}, u32[]{:S(2)}) collective-permute-start(bf16[128,1024]{1,0:T(8,128)(2,1)S(1)} %get-tuple-element.51), channel_id=1, source_target_pairs={{0,1},{1,0},{2,3},{3,2},{4,5},{5,4},{6,7},{7,6},{8,9},{9,8},{10,11... | collective-permute-start | bytes 786440 | tf_op jit(solution)/shard_map/ppermute | solution.py:394
  99.3 16.3 %collective-permute-done.22.refs_2_ = bf16[128,1024]{1,0:T(8,128)(2,1)S(1)} collective-permute-done((bf16[128,1024]{1,0:T(8,128)(2,1)S(1)}, bf16[128,1024]{1,0:T(8,128)(2,1)S(1)}, u32[]{:S(2)}, u32[]{:S(2)}) %collective-permute-start.22) | collective-permute-done | bytes 262176 | tf_op jit(solution)/shard_map/ppermute | solution.py:394
  115.6 0.0 collective-permute-done.23.refs_3_
  115.6 1.4 %add_up.2.refs_4_ = f32[256,1024]{1,0:T(8,128)} custom-call(f32[128,1024]{1,0:T(8,128)S(1)} %get-tuple-element.45.refs_4_.refs_0_, bf16[128,1024]{1,0:T(8,128)(2,1)S(1)} %collective-permute-done.21.refs_1_, bf16[128,1024]{1,0:T(8,128)(2,1)S(1)} %collective-permute-done.22.refs_2_, bf16[128,1024]{1,0:T(8,128)(2,1)S(1)} %collective-permute-done.23.refs_3_), custom_call_target="tpu_custom_call" | custom-call | bytes 1835008 | tf_op jit(solution)/shard_map/add_up/pallas_call | solution.py:365
  117.0 0.0 collective-permute-done.18.refs_1_
  117.0 9.0 %collective-permute-done.19.refs_2_ = bf16[128,1024]{1,0:T(8,128)(2,1)S(1)} collective-permute-done((bf16[128,1024]{1,0:T(8,128)(2,1)S(1)}, bf16[128,1024]{1,0:T(8,128)(2,1)S(1)}, u32[]{:S(2)}, u32[]{:S(2)}) %collective-permute-start.19) | collective-permute-done | bytes 262176 | tf_op jit(solution)/shard_map/ppermute | solution.py:394
  126.1 0.0 collective-permute-done.20.refs_3_
  126.1 1.4 %add_up.3 = f32[256,1024]{1,0:T(8,128)} custom-call(f32[128,1024]{1,0:T(8,128)S(1)} %get-tuple-element.48.refs_0_, bf16[128,1024]{1,0:T(8,128)(2,1)S(1)} %collective-permute-done.18.refs_1_, bf16[128,1024]{1,0:T(8,128)(2,1)S(1)} %collective-permute-done.19.refs_2_, ...), custom_call_target="tpu_custom_call", output_to_operand_aliasing={{}: (4, {})} | custom-call | bytes 1835008 | tf_op jit(solution)/shard_map/add_up/pallas_call | solution.py:365
  (15 shorter events, 0.1 us)
Async XLA Ops:
  0.0 6.3 %copy-start.1 = (bf16[2048,1024]{1,0:T(8,128)(2,1)S(1)}, bf16[2048,1024]{1,0:T(8,128)(2,1)}, u32[]{:S(2)}) copy-start(bf16[2048,1024]{1,0:T(8,128)(2,1)} %refs_2_.1) | copy-start | bytes 12582916
  1.1 6.9 %copy-start.3 = (s32[8]{0:T(128)S(1)}, s32[8]{0:T(128)}, u32[]{:S(2)}) copy-start(s32[8]{0:T(128)} %param.8) | copy-start | bytes 100
  1.1 7.3 %copy-start.2 = (bf16[256,1024]{1,0:T(8,128)(2,1)S(1)}, bf16[256,1024]{1,0:T(8,128)(2,1)}, u32[]{:S(2)}) copy-start(bf16[256,1024]{1,0:T(8,128)(2,1)} %param.5) | copy-start | bytes 1572868
  1.1 1.7 %collective-permute-start.1 = (bf16[256,512]{1,0:T(8,128)(2,1)S(1)}, bf16[256,512]{1,0:T(8,128)(2,1)S(1)}, u32[]{:S(2)}, u32[]{:S(2)}) collective-permute-start(bf16[256,512]{1,0:T(8,128)(2,1)S(1)} %constant_dynamic-slice_fusion.3), channel_id=1, source_target_pairs={{0,4},{4,0},{8,12},{12,8},{16,20},{20,16},{24,28},{28,24},{1,5},{5... | collective-permute-start | bytes 786440 | tf_op jit(solution)/shard_map/ppermute | solution.py:394
  5.9 8.8 %collective-permute-start.3 = (bf16[2048,512]{1,0:T(8,128)(2,1)}, bf16[2048,512]{1,0:T(8,128)(2,1)S(1)}, u32[]{:S(2)}, u32[]{:S(2)}) collective-permute-start(bf16[2048,512]{1,0:T(8,128)(2,1)} %constant_dynamic-slice_fusion.1), channel_id=1, source_target_pairs={{0,4},{4,0},{8,12},{12,8},{16,20},{20,16},{24,28},{28,24},{1,5},{5... | collective-permute-start | bytes 6291464 | tf_op jit(solution)/shard_map/ppermute | solution.py:394
  7.9 9.7 %collective-permute-start.2 = (bf16[2048,512]{1,0:T(8,128)(2,1)}, bf16[2048,512]{1,0:T(8,128)(2,1)}, u32[]{:S(2)}, u32[]{:S(2)}) collective-permute-start(bf16[2048,512]{1,0:T(8,128)(2,1)} %constant_dynamic-slice_fusion.2), channel_id=1, source_target_pairs={{0,4},{4,0},{8,12},{12,8},{16,20},{20,16},{24,28},{28,24},{1,5},{5... | collective-permute-start | bytes 6291464 | tf_op jit(solution)/shard_map/ppermute | solution.py:394
  8.0 2.0 %collective-permute-start = (s32[8]{0:T(128)S(1)}, s32[8]{0:T(128)S(1)}, u32[]{:S(2)}, u32[]{:S(2)}) collective-permute-start(s32[8]{0:T(128)S(1)} %copy-done.3), channel_id=1, source_target_pairs={{0,4},{4,0},{8,12},{12,8},{16,20},{20,16},{24,28},{28,24},{1,5},{5... | collective-permute-start | bytes 104 | tf_op jit(solution)/shard_map/ppermute | solution.py:394
  10.2 22.6 %collective-permute-start.7 = (bf16[256,512]{1,0:T(8,128)(2,1)S(1)}, bf16[256,512]{1,0:T(8,128)(2,1)S(1)}, u32[]{:S(2)}, u32[]{:S(2)}) collective-permute-start(bf16[256,512]{1,0:T(8,128)(2,1)S(1)} %pad_maximum_fusion.refs_0_), channel_id=1, source_target_pairs={{0,24},{4,28},{8,16},{12,20},{16,8},{20,12},{24,0},{28,4},{1,25},{... | collective-permute-start | bytes 786440 | tf_op jit(solution)/shard_map/ppermute | solution.py:394
  14.0 18.8 %collective-permute-start.8 = (bf16[256,512]{1,0:T(8,128)(2,1)S(1)}, bf16[256,512]{1,0:T(8,128)(2,1)S(1)}, u32[]{:S(2)}, u32[]{:S(2)}) collective-permute-start(bf16[256,512]{1,0:T(8,128)(2,1)S(1)} %pad_maximum_fusion.refs_0_), channel_id=1, source_target_pairs={{0,16},{4,20},{8,24},{12,28},{16,0},{20,4},{24,8},{28,12},{1,17},{... | collective-permute-start | bytes 786440 | tf_op jit(solution)/shard_map/ppermute | solution.py:394
  14.5 18.3 %collective-permute-start.9 = (bf16[256,512]{1,0:T(8,128)(2,1)S(1)}, bf16[256,512]{1,0:T(8,128)(2,1)S(1)}, u32[]{:S(2)}, u32[]{:S(2)}) collective-permute-start(bf16[256,512]{1,0:T(8,128)(2,1)S(1)} %pad_maximum_fusion.refs_0_), channel_id=1, source_target_pairs={{0,8},{4,12},{8,0},{12,4},{16,24},{20,28},{24,16},{28,20},{1,9},{5... | collective-permute-start | bytes 786440 | tf_op jit(solution)/shard_map/ppermute | solution.py:394
  14.7 37.9 %collective-permute-start.4 = (bf16[256,512]{1,0:T(8,128)(2,1)S(1)}, bf16[256,512]{1,0:T(8,128)(2,1)S(1)}, u32[]{:S(2)}, u32[]{:S(2)}) collective-permute-start(bf16[256,512]{1,0:T(8,128)(2,1)S(1)} %pad_maximum_fusion.1.refs_1_), channel_id=1, source_target_pairs={{0,24},{4,28},{8,16},{12,20},{16,8},{20,12},{24,0},{28,4},{1,25},{... | collective-permute-start | bytes 786440 | tf_op jit(solution)/shard_map/ppermute | solution.py:394
  17.6 36.1 %collective-permute-start.5 = (bf16[256,512]{1,0:T(8,128)(2,1)S(1)}, bf16[256,512]{1,0:T(8,128)(2,1)S(1)}, u32[]{:S(2)}, u32[]{:S(2)}) collective-permute-start(bf16[256,512]{1,0:T(8,128)(2,1)S(1)} %pad_maximum_fusion.1.refs_1_), channel_id=1, source_target_pairs={{0,16},{4,20},{8,24},{12,28},{16,0},{20,4},{24,8},{28,12},{1,17},{... | collective-permute-start | bytes 786440 | tf_op jit(solution)/shard_map/ppermute | solution.py:394
  32.8 20.9 %collective-permute-start.6 = (bf16[256,512]{1,0:T(8,128)(2,1)S(1)}, bf16[256,512]{1,0:T(8,128)(2,1)S(1)}, u32[]{:S(2)}, u32[]{:S(2)}) collective-permute-start(bf16[256,512]{1,0:T(8,128)(2,1)S(1)} %pad_maximum_fusion.1.refs_1_), channel_id=1, source_target_pairs={{0,8},{4,12},{8,0},{12,4},{16,24},{20,28},{24,16},{28,20},{1,9},{5... | collective-permute-start | bytes 786440 | tf_op jit(solution)/shard_map/ppermute | solution.py:394
  32.8 2.3 %copy-start = (bf16[4,4352,128]{2,1,0:T(8,128)(2,1)S(1)}, bf16[4,4352,128]{2,1,0:T(8,128)(2,1)}, u32[]{:S(2)}) copy-start(bf16[4,4352,128]{2,1,0:T(8,128)(2,1)} %get-tuple-element.34.refs_3_) | copy-start | bytes 13369348
  49.6 21.7 %collective-permute-start.13 = (bf16[272,512]{1,0:T(8,128)(2,1)S(1)}, bf16[272,512]{1,0:T(8,128)(2,1)S(1)}, u32[]{:S(2)}, u32[]{:S(2)}) collective-permute-start(bf16[272,512]{1,0:T(8,128)(2,1)S(1)} %get-tuple-element.36.refs_5_), channel_id=1, source_target_pairs={{0,24},{4,28},{8,16},{12,20},{16,8},{20,12},{24,0},{28,4},{1,25},{... | collective-permute-start | bytes 835592 | tf_op jit(solution)/shard_map/ppermute | solution.py:394
  52.6 19.7 %collective-permute-start.14 = (bf16[272,512]{1,0:T(8,128)(2,1)S(1)}, bf16[272,512]{1,0:T(8,128)(2,1)S(1)}, u32[]{:S(2)}, u32[]{:S(2)}) collective-permute-start(bf16[272,512]{1,0:T(8,128)(2,1)S(1)} %get-tuple-element.41), channel_id=1, source_target_pairs={{0,16},{4,20},{8,24},{12,28},{16,0},{20,4},{24,8},{28,12},{1,17},{... | collective-permute-start | bytes 835592 | tf_op jit(solution)/shard_map/ppermute | solution.py:394
  52.6 21.8 %slice-start = ((s8[8388608]{0:T(1024)(128)(4,1)}), s8[4194304]{0:T(1024)(128)(4,1)S(1)}, s32[]{:S(2)}) async-start(s8[8388608]{0:T(1024)(128)(4,1)} %bitcast.2), calls=%async_computation | async-start | bytes 8388608
  52.6 21.8 %slice-start.1 = ((s8[8388608]{0:T(1024)(128)(4,1)}), s8[4194304]{0:T(1024)(128)(4,1)S(1)}, s32[]{:S(2)}) async-start(s8[8388608]{0:T(1024)(128)(4,1)} %bitcast.2), calls=%async_computation.1 | async-start | bytes 8388608
  52.6 19.7 %collective-permute-start.15 = (bf16[272,512]{1,0:T(8,128)(2,1)S(1)}, bf16[272,512]{1,0:T(8,128)(2,1)S(1)}, u32[]{:S(2)}, u32[]{:S(2)}) collective-permute-start(bf16[272,512]{1,0:T(8,128)(2,1)S(1)} %get-tuple-element.42), channel_id=1, source_target_pairs={{0,8},{4,12},{8,0},{12,4},{16,24},{20,28},{24,16},{28,20},{1,9},{5... | collective-permute-start | bytes 835592 | tf_op jit(solution)/shard_map/ppermute | solution.py:394
  68.8 12.1 %collective-permute-start.10 = (bf16[272,512]{1,0:T(8,128)(2,1)S(1)}, bf16[272,512]{1,0:T(8,128)(2,1)S(1)}, u32[]{:S(2)}, u32[]{:S(2)}) collective-permute-start(bf16[272,512]{1,0:T(8,128)(2,1)S(1)} %get-tuple-element.37.refs_4_), channel_id=1, source_target_pairs={{0,24},{4,28},{8,16},{12,20},{16,8},{20,12},{24,0},{28,4},{1,25},{... | collective-permute-start | bytes 835592 | tf_op jit(solution)/shard_map/ppermute | solution.py:394
  71.3 11.2 %collective-permute-start.11 = (bf16[272,512]{1,0:T(8,128)(2,1)S(1)}, bf16[272,512]{1,0:T(8,128)(2,1)S(1)}, u32[]{:S(2)}, u32[]{:S(2)}) collective-permute-start(bf16[272,512]{1,0:T(8,128)(2,1)S(1)} %get-tuple-element.38), channel_id=1, source_target_pairs={{0,16},{4,20},{8,24},{12,28},{16,0},{20,4},{24,8},{28,12},{1,17},{... | collective-permute-start | bytes 835592 | tf_op jit(solution)/shard_map/ppermute | solution.py:394
  71.3 11.4 %collective-permute-start.12 = (bf16[272,512]{1,0:T(8,128)(2,1)S(1)}, bf16[272,512]{1,0:T(8,128)(2,1)S(1)}, u32[]{:S(2)}, u32[]{:S(2)}) collective-permute-start(bf16[272,512]{1,0:T(8,128)(2,1)S(1)} %get-tuple-element.39), channel_id=1, source_target_pairs={{0,8},{4,12},{8,0},{12,4},{16,24},{20,28},{24,16},{28,20},{1,9},{5... | collective-permute-start | bytes 835592 | tf_op jit(solution)/shard_map/ppermute | solution.py:394
  73.0 1.4 %collective-permute-start.16 = (bf16[128,512]{1,0:T(8,128)(2,1)S(1)}, bf16[128,512]{1,0:T(8,128)(2,1)S(1)}, u32[]{:S(2)}, u32[]{:S(2)}) collective-permute-start(bf16[128,512]{1,0:T(8,128)(2,1)S(1)} %get-tuple-element.44), channel_id=1, source_target_pairs={{0,4},{4,0},{8,12},{12,8},{16,20},{20,16},{24,28},{28,24},{1,5},{5... | collective-permute-start | bytes 393224 | tf_op jit(solution)/shard_map/ppermute | solution.py:394
  77.2 14.9 %collective-permute-start.21 = (bf16[128,1024]{1,0:T(8,128)(2,1)S(1)}, bf16[128,1024]{1,0:T(8,128)(2,1)S(1)}, u32[]{:S(2)}, u32[]{:S(2)}) collective-permute-start(bf16[128,1024]{1,0:T(8,128)(2,1)S(1)} %get-tuple-element.52), channel_id=1, source_target_pairs={{0,3},{1,2},{2,1},{3,0},{4,7},{5,6},{6,5},{7,4},{8,11},{9,10},{10,... | collective-permute-start | bytes 786440 | tf_op jit(solution)/shard_map/ppermute | solution.py:394
  83.3 4.3 %collective-permute-start.17 = (bf16[128,512]{1,0:T(8,128)(2,1)S(1)}, bf16[128,512]{1,0:T(8,128)(2,1)S(1)}, u32[]{:S(2)}, u32[]{:S(2)}) collective-permute-start(bf16[128,512]{1,0:T(8,128)(2,1)S(1)} %get-tuple-element.47), channel_id=1, source_target_pairs={{0,4},{4,0},{8,12},{12,8},{16,20},{20,16},{24,28},{28,24},{1,5},{5... | collective-permute-start | bytes 393224 | tf_op jit(solution)/shard_map/ppermute | solution.py:394
  83.4 32.2 %collective-permute-start.22 = (bf16[128,1024]{1,0:T(8,128)(2,1)S(1)}, bf16[128,1024]{1,0:T(8,128)(2,1)S(1)}, u32[]{:S(2)}, u32[]{:S(2)}) collective-permute-start(bf16[128,1024]{1,0:T(8,128)(2,1)S(1)} %get-tuple-element.53), channel_id=1, source_target_pairs={{0,2},{1,3},{2,0},{3,1},{4,6},{5,7},{6,4},{7,5},{8,10},{9,11},{10,... | collective-permute-start | bytes 786440 | tf_op jit(solution)/shard_map/ppermute | solution.py:394
  86.1 29.6 %collective-permute-start.23 = (bf16[128,1024]{1,0:T(8,128)(2,1)S(1)}, bf16[128,1024]{1,0:T(8,128)(2,1)S(1)}, u32[]{:S(2)}, u32[]{:S(2)}) collective-permute-start(bf16[128,1024]{1,0:T(8,128)(2,1)S(1)} %get-tuple-element.54), channel_id=1, source_target_pairs={{0,1},{1,0},{2,3},{3,2},{4,5},{5,4},{6,7},{7,6},{8,9},{9,8},{10,11... | collective-permute-start | bytes 786440 | tf_op jit(solution)/shard_map/ppermute | solution.py:394
  90.2 26.8 %collective-permute-start.18 = (bf16[128,1024]{1,0:T(8,128)(2,1)S(1)}, bf16[128,1024]{1,0:T(8,128)(2,1)S(1)}, u32[]{:S(2)}, u32[]{:S(2)}) collective-permute-start(bf16[128,1024]{1,0:T(8,128)(2,1)S(1)} %get-tuple-element.49), channel_id=1, source_target_pairs={{0,3},{1,2},{2,1},{3,0},{4,7},{5,6},{6,5},{7,4},{8,11},{9,10},{10,... | collective-permute-start | bytes 786440 | tf_op jit(solution)/shard_map/ppermute | solution.py:394
  91.0 35.1 %collective-permute-start.19 = (bf16[128,1024]{1,0:T(8,128)(2,1)S(1)}, bf16[128,1024]{1,0:T(8,128)(2,1)S(1)}, u32[]{:S(2)}, u32[]{:S(2)}) collective-permute-start(bf16[128,1024]{1,0:T(8,128)(2,1)S(1)} %get-tuple-element.50), channel_id=1, source_target_pairs={{0,2},{1,3},{2,0},{3,1},{4,6},{5,7},{6,4},{7,5},{8,10},{9,11},{10,... | collective-permute-start | bytes 786440 | tf_op jit(solution)/shard_map/ppermute | solution.py:394
  92.2 33.9 %collective-permute-start.20 = (bf16[128,1024]{1,0:T(8,128)(2,1)S(1)}, bf16[128,1024]{1,0:T(8,128)(2,1)S(1)}, u32[]{:S(2)}, u32[]{:S(2)}) collective-permute-start(bf16[128,1024]{1,0:T(8,128)(2,1)S(1)} %get-tuple-element.51), channel_id=1, source_target_pairs={{0,1},{1,0},{2,3},{3,2},{4,5},{5,4},{6,7},{7,6},{8,9},{9,8},{10,11... | collective-permute-start | bytes 786440 | tf_op jit(solution)/shard_map/ppermute | solution.py:394
